TPU v7x, 32 devices: a whole 2x2x4 slice. The times are simulated.
32 devices in a mesh: rep: 4 (over z), fsdp: 4 (over y, core), expert: 2 (over x).
Axes of the slice: x: 2, y: 2, z: 4, core: 2. Of those that a mesh axis runs over, the one named last changes fastest.
Arguments:
- tokens: bfloat16 [32768, 768], P(('rep', 'fsdp', 'expert')), may hold values from -6 to 6
- segment_ids: int32 [32, 1024], P(('rep', 'fsdp', 'expert')), may hold values from 0 to 3, never falling along the last dimension, each value on 1 to 512 neighbouring positions
- offset_bucket: int32 [2047], replicated, may hold values from 0 to 31
- routes: int32 [32768, 1], P(('rep', 'fsdp', 'expert')), may hold values from 0 to 1; in each aligned block of 1024 rows (0 to 1023, 1024 to 2047, ...) at most 640 rows name the same one
- capacity_keep: int32 [32768], P(('rep', 'fsdp', 'expert')), may hold values 0 or 1
- gain_attn: bfloat16 [768], P(('fsdp', 'expert')), may hold values from 0.5 to 1.5
- gain_ffn: bfloat16 [768], P(('fsdp', 'expert')), may hold values from 0.5 to 1.5
- w_query: bfloat16 [768, 768], P(('fsdp', 'expert')), may hold values from -0.21875 to 0.21875
- w_key: bfloat16 [768, 768], P(('fsdp', 'expert')), may hold values from -0.21875 to 0.21875
- w_value: bfloat16 [768, 768], P(('fsdp', 'expert')), may hold values from -0.21875 to 0.21875
- w_output: bfloat16 [768, 768], P(('fsdp', 'expert')), may hold values from -0.875 to 0.875
- rel_table: bfloat16 [32, 12], P(('fsdp', 'expert')), may hold values from -4 to 4
- router: bfloat16 [768, 2], P(('fsdp', 'expert')), may hold values from -0.21875 to 0.21875
- expert_in: bfloat16 [2, 768, 3072], P('expert'), may hold values from -0.21875 to 0.21875
- expert_out: bfloat16 [2, 3072, 768], P('expert'), may hold values from -0.21875 to 0.21875
- grad_out: bfloat16 [32768, 768], P(('rep', 'fsdp', 'expert')), may hold values from -6 to 6
Outputs:
- block_output: bfloat16 [32768, 768], P(('rep', 'fsdp', 'expert'))
- grad_tokens: bfloat16 [32768, 768], P(('rep', 'fsdp', 'expert'))
- grad_gain_attn: float32 [768], P(('fsdp', 'expert'))
- grad_gain_ffn: float32 [768], P(('fsdp', 'expert'))
- grad_w_query: float32 [768, 768], P(('fsdp', 'expert'))
- grad_w_key: float32 [768, 768], P(('fsdp', 'expert'))
- grad_w_value: float32 [768, 768], P(('fsdp', 'expert'))
- grad_w_output: float32 [768, 768], P(('fsdp', 'expert'))
- grad_rel_table: float32 [32, 12], P(('fsdp', 'expert'))
- grad_router: float32 [768, 2], P(('fsdp', 'expert'))
- grad_expert_in: float32 [2, 768, 3072], P('expert')
- grad_expert_out: float32 [2, 3072, 768], P('expert')
Inputs may be any that keep to these rules, and one draw needn't show every extreme that they name: `routes`: in the rows of one device no expert is named more than 640 times. `segment_ids`: numbers never fall along a sequence; a document has at most 512 positions.
All inputs are finite; a program needn't handle non-finite values. No bound on the sum of `capacity_keep` on one device may be relied on, other than what follows from the above.
Results may differ from a plain program's by a relative error of at most 0.015.
Values may be sent and summed in bfloat16 or wider, within the bound.
No kernel may reach another device: no remote copies, remote signals or barrier semaphores. Data moves between devices by JAX's collectives and lax.ppermute only.
A program may use at most 896 MiB of HBM per device.

v0:
```python
import functools

import jax
import jax.numpy as jnp
from jax import lax
from jax.experimental import pallas as pl
from jax.experimental.pallas import tpu as pltpu
from jax.sharding import PartitionSpec as P

F32=jnp.float32; BF=jnp.bfloat16
ROWS=256
def dot_t(a,b):
    return lax.dot_general(a,b,(((1,),(1,)),((),())),preferred_element_type=F32)
def dot_n(a,b):
    return lax.dot_general(a,b,(((1,),(0,)),((),())),preferred_element_type=F32)

def attn_fwd_kernel(scaling, head, q_ref,k_ref,v_ref,sq_ref,sk_ref,off_ref,o_ref,p_ref,bias):
    length=q_ref.shape[0]; wide=off_ref.shape[-1]
    lane=lax.broadcasted_iota(jnp.int32,(1,2*head),1)
    kext=jnp.concatenate([k_ref[...],sk_ref[...]],axis=1)
    outs=[None]*(length//ROWS)
    for hh in range(2):
        mine=(lane>=head*hh)&(lane<head*(hh+1))
        spread=jnp.broadcast_to(off_ref[0,hh:hh+1,:],(ROWS,wide))
        bias[...]=pltpu.roll(spread,wide-(ROWS-1),1,stride=1,stride_axis=0)
        for b in range(length//ROWS):
            rows=pl.ds(b*ROWS,ROWS)
            qm=jnp.where(mine,q_ref[rows,:].astype(F32)*scaling,0.0).astype(BF)
            s=dot_t(jnp.concatenate([qm,sq_ref[rows,:]],axis=1),kext)
            s=s+bias[:,length-ROWS-b*ROWS:2*length-ROWS-b*ROWS]
            m=jnp.max(s,axis=-1,keepdims=True)
            e=jnp.exp(s-m)
            inv=1.0/jnp.sum(e,axis=-1,keepdims=True)
            p=(e*inv).astype(BF)
            p_ref[0,hh,rows,:]=p
            o=dot_n(p,v_ref[...])
            if hh==0: outs[b]=o
            else: o_ref[rows,:]=jnp.where(mine,o,outs[b]).astype(BF)

def attn_fwd(qkv,sq,sk,off,heads,head):
    length=qkv.shape[0]; pairs=heads//2
    wide=off.shape[-1]
    return pl.pallas_call(functools.partial(attn_fwd_kernel,head**-0.5,head),
        grid=(pairs,),
        in_specs=[pl.BlockSpec((length,2*head),lambda p:(0,p)),
                  pl.BlockSpec((length,2*head),lambda p:(0,pairs+p)),
                  pl.BlockSpec((length,2*head),lambda p:(0,2*pairs+p)),
                  pl.BlockSpec((length,128),lambda p:(0,0)),
                  pl.BlockSpec((length,128),lambda p:(0,0)),
                  pl.BlockSpec((1,2,wide),lambda p:(p,0,0))],
        out_specs=[pl.BlockSpec((length,2*head),lambda p:(0,p)),
                   pl.BlockSpec((1,2,length,length),lambda p:(p,0,0,0))],
        out_shape=[jax.ShapeDtypeStruct((length,heads*head),BF),jax.ShapeDtypeStruct((pairs,2,length,length),BF)],
        scratch_shapes=[pltpu.VMEM((ROWS,wide),F32)],
        compiler_params=pltpu.CompilerParams(vmem_limit_bytes=56*2**20),
        name="attn_fwd",
    )(qkv,qkv,qkv,sq,sk,off)

def attn_bwd_kernel(scaling, head, q_ref,k_ref,v_ref,do_ref,o_ref,p_ref,dq_ref,dk_ref,dv_ref,doff_ref,acc):
    length=q_ref.shape[0]; wide=acc.shape[-1]
    lane=lax.broadcasted_iota(jnp.int32,(1,2*head),1)
    extra=jnp.where(lax.broadcasted_iota(jnp.int32,(length,128),1)<2,1.0,0.0).astype(BF)
    vext=jnp.concatenate([v_ref[...],extra],axis=1)
    lane_b=lax.broadcasted_iota(jnp.int32,(ROWS,128),1)
    dqs=[None]*(length//ROWS)
    dks=[];dvs=[]
    for hh in range(2):
        mine=(lane>=head*hh)&(lane<head*(hh+1))
        acc[...]=jnp.zeros_like(acc)
        dk=jnp.zeros((head,length),F32); dv=jnp.zeros((head,length),F32)
        for b in range(length//ROWS):
            rows=pl.ds(b*ROWS,ROWS)
            do=do_ref[rows,:]
            dom=jnp.where(mine,do.astype(F32),0.0)
            delta=-jnp.sum(dom*o_ref[rows,:].astype(F32),axis=-1,keepdims=True)
            hi=delta.astype(BF).astype(F32)
            ext=jnp.where(lane_b==0,hi,jnp.where(lane_b==1,delta-hi,0.0)).astype(BF)
            dp=dot_t(jnp.concatenate([dom.astype(BF),ext],axis=1),vext)
            p=p_ref[0,hh,rows,:]
            ds=p.astype(F32)*dp
            at=length-ROWS-b*ROWS
            acc[:,at:at+length]+=ds
            dsb=ds.astype(BF)
            dq=dot_n(dsb,k_ref[...])
            if hh==0: dqs[b]=dq
            else: dq_ref[rows,:]=(jnp.where(mine,dq,dqs[b])*scaling).astype(BF)
            qt=q_ref[rows,:].T[hh*head:(hh+1)*head]
            dot_=do.T[hh*head:(hh+1)*head]
            dk+=dot_n(qt,dsb)
            dv+=dot_n(dot_,p)
        dks.append(dk); dvs.append(dv)
        x=acc[...]
        n=ROWS
        while n>8:
            n//=2
            x=x[:n]+pltpu.roll(x[n:],wide-n,1)
        row=lax.broadcasted_iota(jnp.int32,x.shape,0)
        for bit in (4,2,1):
            x=jnp.where((row&bit)!=0,pltpu.roll(x,wide-bit,1),x)
        doff_ref[0,hh:hh+1,:]=pltpu.roll(jnp.broadcast_to(jnp.sum(x,axis=0,keepdims=True),(8,wide)),ROWS-1,1)[:1]
    dk_ref[...]=(jnp.concatenate(dks,axis=0).T*scaling).astype(BF)
    dv_ref[...]=jnp.concatenate(dvs,axis=0).T.astype(BF)

def attn_bwd(qkv,do,o,p,wide,heads,head):
    length=qkv.shape[0]; pairs=heads//2
    col=lambda at: pl.BlockSpec((length,2*head),lambda p:(0,at+p))
    return pl.pallas_call(functools.partial(attn_bwd_kernel,head**-0.5,head),
        grid=(pairs,),
        in_specs=[col(0),col(pairs),col(2*pairs),col(0),col(0),
                  pl.BlockSpec((1,2,length,length),lambda p:(p,0,0,0))],
        out_specs=[col(0),col(0),col(0),pl.BlockSpec((1,2,wide),lambda p:(p,0,0))],
        out_shape=[jax.ShapeDtypeStruct((length,heads*head),BF)]*3+[jax.ShapeDtypeStruct((pairs,2,wide),F32)],
        scratch_shapes=[pltpu.VMEM((ROWS,wide),F32)],
        compiler_params=pltpu.CompilerParams(vmem_limit_bytes=56*2**20),
        name="attn_bwd",
    )(qkv,qkv,qkv,do,o,p)
FB=512
def gelu_pair(u):
    c=0.7978845608028654
    sq=u*u
    t=jnp.tanh(c*(u+0.044715*(u*sq)))
    half=0.5*(1.0+t)
    return u*half, half+0.5*u*(1.0-t*t)*(c+(3.0*0.044715*c)*sq)

def expert_kernel(experts,x_ref,g_ref,router_ref,mine_ref,win_ref,wout_ref,
                  geo_ref,dn_ref,act_ref,du_ref,deo_ref,drouter_ref,eo,dx,gate):
    step=pl.program_id(0); last=pl.num_programs(0)-1
    def probabilities():
        logits=dot_n(x_ref[...],router_ref[...])
        lane=lax.broadcasted_iota(jnp.int32,logits.shape,1)
        logits=jnp.where(lane<experts,logits,-1e30)
        e=jnp.exp(logits-jnp.max(logits,axis=-1,keepdims=True))
        return e/jnp.sum(e,axis=-1,keepdims=True)
    @pl.when(step==0)
    def _():
        chosen=jnp.sum(probabilities()*mine_ref[...],axis=-1,keepdims=True)
        gate[...]=jnp.broadcast_to(chosen,gate.shape)
        deo_ref[...]=(chosen*g_ref[...].astype(F32)).astype(BF)
        eo[...]=jnp.zeros_like(eo); dx[...]=jnp.zeros_like(dx)
    u=dot_n(x_ref[...],win_ref[0])
    dact=dot_t(deo_ref[...],wout_ref[0])
    a,slope=gelu_pair(u)
    a=a.astype(BF)
    d=(dact*slope).astype(BF)
    act_ref[...]=a; du_ref[...]=d
    eo[...]+=dot_n(a,wout_ref[0])
    dx[...]+=dot_t(d,win_ref[0])
    @pl.when(step==last)
    def _():
        made=eo[...].astype(BF).astype(F32)
        chosen=gate[:,:1]
        geo_ref[...]=(chosen*made).astype(BF)
        dgate=jnp.sum(made*g_ref[...].astype(F32),axis=-1,keepdims=True)
        probs=probabilities()
        dprobs=mine_ref[...]*dgate
        dlog=(probs*(dprobs-jnp.sum(probs*dprobs,axis=-1,keepdims=True))).astype(BF)
        dn_ref[...]=(dx[...]+dot_t(dlog,router_ref[...])).astype(BF)
        drouter_ref[...]=dot_n(dlog.T,x_ref[...])

def expert(x,g,router,mine,win,wout,experts):
    rows,width=x.shape; ff=win.shape[-1]
    fixed=lambda shape: pl.BlockSpec(shape,lambda f:(0,)*len(shape))
    return pl.pallas_call(functools.partial(expert_kernel,experts),
        grid=(ff//FB,),
        in_specs=[fixed((rows,width)),fixed((rows,width)),fixed((width,128)),fixed((1,128)),
                  pl.BlockSpec((1,width,FB),lambda f:(0,0,f)),pl.BlockSpec((1,FB,width),lambda f:(0,f,0))],
        out_specs=[fixed((rows,width)),fixed((rows,width)),pl.BlockSpec((rows,FB),lambda f:(0,f)),
                   pl.BlockSpec((rows,FB),lambda f:(0,f)),fixed((rows,width)),fixed((128,width))],
        out_shape=[jax.ShapeDtypeStruct((rows,width),BF),jax.ShapeDtypeStruct((rows,width),BF),
                   jax.ShapeDtypeStruct((rows,ff),BF),jax.ShapeDtypeStruct((rows,ff),BF),
                   jax.ShapeDtypeStruct((rows,width),BF),jax.ShapeDtypeStruct((128,width),F32)],
        scratch_shapes=[pltpu.VMEM((rows,width),F32),pltpu.VMEM((rows,width),F32),pltpu.VMEM((rows,128),F32)],
        compiler_params=pltpu.CompilerParams(vmem_limit_bytes=56*2**20),
        cost_estimate=pl.CostEstimate(flops=8*rows*width*ff,bytes_accessed=4*width*ff+4*rows*ff,transcendentals=rows*ff),
        name="expert",
    )(x,g,router,mine,win,wout)

def weights_kernel(parts,*refs):
    xs,deos,acts,dus=(refs[i*parts:(i+1)*parts] for i in range(4))
    din_ref,dout_ref=refs[4*parts:4*parts+2]; turned=refs[4*parts+2:]
    @pl.when(pl.program_id(0)==0)
    def _():
        for t,x in zip(turned,xs): t[...]=x[...].T
    din=dout=None
    for t,deo,act,du in zip(turned,deos,acts,dus):
        a=dot_n(t[...],du[...])
        b=lax.dot_general(act[...],deo[...],(((0,),(0,)),((),())),preferred_element_type=F32)
        din=a if din is None else din+a
        dout=b if dout is None else dout+b
    din_ref[...]=din.astype(din_ref.dtype)
    dout_ref[...]=dout.astype(dout_ref.dtype)

def expert_weights(xs,deos,acts,dus,kind):
    width=xs[0].shape[1]; ff=acts[0].shape[1]; parts=len(xs)
    total=sum(x.shape[0] for x in xs)
    fixed=lambda shape: pl.BlockSpec(shape,lambda f:(0,)*len(shape))
    return pl.pallas_call(functools.partial(weights_kernel,parts),
        grid=(ff//FB,),
        in_specs=[fixed(x.shape) for x in xs]+[fixed(x.shape) for x in deos]
                 +[pl.BlockSpec((a.shape[0],FB),lambda f:(0,f)) for a in acts]
                 +[pl.BlockSpec((a.shape[0],FB),lambda f:(0,f)) for a in dus],
        out_specs=[pl.BlockSpec((width,FB),lambda f:(0,f)),pl.BlockSpec((FB,width),lambda f:(f,0))],
        out_shape=[jax.ShapeDtypeStruct((width,ff),kind),jax.ShapeDtypeStruct((ff,width),kind)],
        scratch_shapes=[pltpu.VMEM((width,x.shape[0]),BF) for x in xs],
        compiler_params=pltpu.CompilerParams(vmem_limit_bytes=56*2**20),
        cost_estimate=pl.CostEstimate(flops=4*total*width*ff,bytes_accessed=4*width*ff+4*total*ff,transcendentals=0),
        name="expert_weights",
    )(*xs,*deos,*acts,*dus)
EPS = 1e-06
NEG = -1e30
HIGH = lax.Precision.HIGHEST
GROUP = ("fsdp", "expert")


def normalize(values, gain):
    row_scale = lax.rsqrt(jnp.mean(values * values, axis=-1, keepdims=True) + EPS)
    return (values * row_scale * gain, row_scale)


def normalize_back(values, row_scale, gain, cotangent):
    weighted = cotangent * gain
    d_gain = jnp.sum(cotangent * values * row_scale, axis=0)
    d_values = row_scale * weighted - values * row_scale**3 * jnp.mean(
        weighted * values, axis=-1, keepdims=True
    )
    return (d_values, d_gain)


def dot32(left, right):
    return jnp.dot(left, right, preferred_element_type=F32)


def swap(blocks, sign, experts):
    moved = [
        lax.ppermute(block, "expert", [(i, (i + sign * (at + 1)) % experts) for i in range(experts)])
        for at, block in enumerate(blocks)
    ]
    return moved


def after(value, earlier):
    return lax.optimization_barrier((value, earlier))[0]


def body(
    group_size,
    tokens,
    segment_ids,
    offset_bucket,
    routes,
    capacity_keep,
    gain_attn,
    gain_ffn,
    w_query,
    w_key,
    w_value,
    w_output,
    rel_table,
    router,
    expert_in,
    expert_out,
    grad_out,
):
    length = segment_ids.shape[1]
    heads = rel_table.shape[1]
    inner = w_query.shape[1]
    head = inner // heads
    experts = router.shape[1]
    token_rows, width = tokens.shape
    capacity = token_rows * 5 // (4 * experts)
    slots = experts * capacity
    shard = w_query.shape[0]
    own_buckets = rel_table.shape[0]
    buckets = own_buckets * group_size
    me = lax.axis_index("expert")

    small_cols = [
        gain_attn[:, None],
        gain_ffn[:, None],
        router,
        jnp.pad(rel_table, ((0, shard - own_buckets), (0, 0))),
    ]
    used = 2 + experts + heads
    packed = jnp.concatenate(
        [w_query, w_key, w_value] + small_cols + [jnp.zeros((shard, -used % 128), BF)], axis=1
    )
    gathered = lax.all_gather(packed, GROUP, axis=0, tiled=True)
    proj_in = gathered[:, : 3 * inner]
    small = gathered[:, 3 * inner :]
    gain_one = small[:, 0].astype(F32)
    gain_two = small[:, 1].astype(F32)
    route_weight = small[:, 2 : 2 + experts]
    table = small[:, 2 + experts : used].reshape(group_size, shard, heads)[:, :own_buckets]
    table = table.reshape(buckets, heads)
    proj_output = lax.all_gather(after(w_output, gathered), GROUP, axis=0, tiled=True)

    chosen = routes[:, 0]
    picked = (chosen[:, None] == jnp.arange(experts, dtype=jnp.int32)[None, :]).astype(jnp.int32)
    earlier = jnp.cumsum(picked, axis=0) - picked
    slot = lax.rem(chosen - me + experts, experts) * capacity + jnp.sum(earlier * picked, axis=-1)
    slot = jnp.where(capacity_keep == 1, slot, slots)
    slot_ids = jnp.arange(slots, dtype=jnp.int32)
    to_slots = (slot_ids[:, None] == slot[None, :]).astype(BF)
    to_tokens = (slot[:, None] == slot_ids[None, :]).astype(BF)

    def leave(values, first, last):
        return dot32(to_slots[first:last], values).astype(BF)

    def depart(values):
        return [leave(values, s * capacity, (s + 1) * capacity) for s in range(1, experts)]

    g_local = leave(grad_out, 0, capacity)
    g_remote = jnp.concatenate(
        swap([after(block, gathered) for block in depart(grad_out)], 1, experts), axis=0
    )

    inputs = tokens.astype(F32)
    normed, scale_one = normalize(inputs, gain_one)
    normed_low = normed.astype(BF)
    qkv = dot32(normed_low, proj_in).astype(BF)

    bucket_of = jnp.concatenate([offset_bucket, jnp.full((1,), -1, jnp.int32)])
    hits = (bucket_of[None, :] == jnp.arange(buckets, dtype=jnp.int32)[:, None]).astype(BF)
    offsets = dot32(table.T, hits).reshape(heads // 2, 2, 2 * length)
    same = segment_ids[0][:, None] == jnp.arange(128, dtype=jnp.int32)[None, :]
    seg_q = jnp.where(same, 0.0, NEG).astype(BF)
    seg_k = same.astype(BF)
    attn_out, weights = attn_fwd(qkv, seg_q, seg_k, offsets, heads, head)

    resid = inputs + dot32(attn_out, proj_output)
    normed_two, scale_two = normalize(resid, gain_two)
    second_low = normed_two.astype(BF)

    x_remote = jnp.concatenate(swap(depart(second_low), 1, experts), axis=0)
    x_local = leave(second_low, 0, capacity)
    route_wide = jnp.pad(route_weight, ((0, 0), (0, 128 - experts)))
    mine = (jnp.arange(128, dtype=jnp.int32) == me).astype(F32)[None, :]
    geo_l, dn_l, act_l, du_l, deo_l, dr_l = expert(
        x_local, g_local, route_wide, mine, expert_in, expert_out, experts
    )
    geo_r, dn_r, act_r, du_r, deo_r, dr_r = expert(
        x_remote, g_remote, route_wide, mine, expert_in, expert_out, experts
    )

    def cut(rows):
        return [rows[s * capacity : (s + 1) * capacity] for s in range(experts - 1)]

    dn_back = swap(cut(dn_r), -1, experts)
    d_in, d_out = expert_weights([x_local, x_remote], [deo_l, deo_r], [act_l, act_r], [du_l, du_r], BF)
    sum_in, sum_out = lax.psum((d_in, d_out), ("rep", "fsdp"))
    d_second = dot32(to_tokens, jnp.concatenate([dn_l] + dn_back, axis=0))
    geo_back = swap(cut(after(geo_r, dn_back[-1])), -1, experts)
    output = resid + dot32(to_tokens, jnp.concatenate([geo_l] + geo_back, axis=0))
    output = output.astype(BF)
    d_router = (dr_l + dr_r)[:experts].T

    cotangent = grad_out.astype(F32)
    d_resid_norm, d_gain_two = normalize_back(resid, scale_two, gain_two, d_second)
    d_resid = cotangent + d_resid_norm
    d_branch = d_resid.astype(BF)
    d_attn = dot_t(d_branch, proj_output).astype(BF)
    d_proj_output = lax.dot_general(
        attn_out, d_branch, (((0,), (0,)), ((), ())), preferred_element_type=F32
    ).astype(BF)
    d_query, d_key, d_value, d_offsets = attn_bwd(
        qkv, d_attn, attn_out, weights, 2 * length, heads, head
    )
    d_table = jnp.dot(
        hits.astype(F32), d_offsets.reshape(heads, 2 * length).T, precision=HIGH
    )
    d_qkv = jnp.concatenate([d_query, d_key, d_value], axis=1)
    d_proj = lax.dot_general(
        normed_low, d_qkv, (((0,), (0,)), ((), ())), preferred_element_type=F32
    ).astype(BF)
    d_normed = dot_t(d_qkv, proj_in)
    d_input_norm, d_gain_one = normalize_back(inputs, scale_one, gain_one, d_normed)
    grad_tokens = (d_resid + d_input_norm).astype(BF)

    share_out = lax.psum_scatter(d_proj_output, GROUP, scatter_dimension=0, tiled=True)
    share_in = lax.psum_scatter(d_proj, GROUP, scatter_dimension=0, tiled=True)
    d_small = jnp.concatenate(
        [
            d_gain_one[:, None],
            d_gain_two[:, None],
            d_router,
            jnp.pad(
                d_table.reshape(group_size, own_buckets, heads),
                ((0, 0), (0, shard - own_buckets), (0, 0)),
            ).reshape(width, heads),
            jnp.zeros((width, -used % 128), F32),
        ],
        axis=1,
    )
    share_small = lax.psum_scatter(d_small, GROUP, scatter_dimension=0, tiled=True)
    share_out, share_in, share_small = lax.psum((share_out, share_in, share_small), "rep")
    share_in = share_in.astype(F32)
    return (
        output,
        grad_tokens,
        share_small[:, 0],
        share_small[:, 1],
        share_in[:, :inner],
        share_in[:, inner : 2 * inner],
        share_in[:, 2 * inner :],
        share_out.astype(F32),
        share_small[:own_buckets, 2 + experts : used],
        share_small[:, 2 : 2 + experts],
        sum_in.astype(F32)[None],
        sum_out.astype(F32)[None],
    )


def solution(mesh):
    rows, group = P(("rep", "fsdp", "expert"), None), P(("fsdp", "expert"), None)
    flat_rows, flat_group = P(("rep", "fsdp", "expert")), P(("fsdp", "expert"))
    whole = P("expert", None, None)
    group_size = mesh.shape["fsdp"] * mesh.shape["expert"]
    return jax.shard_map(
        functools.partial(body, group_size),
        mesh=mesh,
        in_specs=(
            rows, rows, P(), rows, flat_rows, flat_group, flat_group,
            group, group, group, group, group, group, whole, whole, rows,
        ),
        out_specs=(
            rows, rows, flat_group, flat_group,
            group, group, group, group, group, group, whole, whole,
        ),
        check_vma=False,
    )
```

profile of v0, /device:TPU:8, one launch (start us, length us, event | category | flops | bytes accessed | tf_op | source)
XLA Modules:
  0.0 603.0 jit_solution(13898476160661746795)
XLA Ops:
  7.2 0.8 copy.77
  8.0 0.8 copy.78
  8.8 0.8 copy.79
  9.6 0.7 pad.12
  10.3 1.9 concatenate.18
  12.3 1.7 copy.76
  14.0 0.6 reduce-window.6
  15.0 1.7 copy.84
  17.3 0.6 multiply_multiply_fusion
  17.9 0.9 select_convert_fusion.sq_ref
  18.8 0.9 fusion.47.sk_ref
  19.8 28.6 %all-gather.3.cloned.1.call-done = bf16[768,2432]{1,0:T(8,128)(2,1)} async-done(((bf16[96,2432]{1,0:T(8,128)(2,1)}), bf16[768,2432]{1,0:T(8,128)(2,1)}) %all-gather.3.cloned.1.call-update) | async-done | bytes 3735568 | tf_op jit(solution)/shard_map/all_gather | solution.py:287
  48.4 1.1 iota_compare_fusion
  49.5 4.0 fusion.42
  53.5 1.0 slice.81
  54.8 0.7 copy.82.off_ref
  55.5 1.5 collective-permute-start.1
  57.0 1.3 convert_reduce_fusion
  58.3 7.8 %convolution_convert_fusion.q_ref.k_ref.v_ref = bf16[1024,2304]{1,0:T(8,128)(2,1)} fusion(bf16[768,2432]{1,0:T(8,128)(2,1)} %all-gather.3.cloned.1.call-done, bf16[1024,768]{0,1:T(8,128)(2,1)S(1)} %copy.76, f32[768]{0:T(1024)S(1)} %get-tuple-element.111, f32[1024]{0:T(1024)S(1)} %get-tuple-element.122), kind=kOutput, calls=%fused_computation.6 | convolution fusion | flops 3629383680 | bytes 9837568 | tf_op jit(solution)/shard_map/dot_general | solution.py:230
  66.1 36.1 %attn_fwd.1 = (bf16[1024,768]{1,0:T(8,128)(2,1)}, bf16[6,2,1024,1024]{3,2,1,0:T(8,128)(2,1)}) custom-call(bf16[1024,2304]{1,0:T(8,128)(2,1)} %convolution_convert_fusion.q_ref.k_ref.v_ref, bf16[1024,2304]{1,0:T(8,128)(2,1)} %convolution_convert_fusion.q_ref.k_ref.v_ref, bf16[1024,2304]{1,0:T(8,128)(2,1)} %convolution_convert_fusion.q_ref.k_ref.v_ref, ...), custom_call_target="tpu_custom_call" | custom-call | tf_op jit(solution)/shard_map/attn_fwd/pallas_call | solution.py:43
  102.2 3.4 multiply_reduce_fusion.2
  105.7 1.5 fusion.39
  107.2 0.7 collective-permute-start
  108.4 0.6 multiply_add_fusion
  109.0 2.3 fusion.36.g_ref
  111.2 1.0 slice.86
  112.3 0.7 pad.13.router_ref
  113.0 2.4 fusion.33.x_ref.refs_0_
  115.4 15.6 %collective-permute-done.x_ref.refs_1_ = bf16[640,768]{1,0:T(8,128)(2,1)} collective-permute-done((bf16[640,768]{1,0:T(8,128)(2,1)S(1)}, bf16[640,768]{1,0:T(8,128)(2,1)}, u32[]{:S(2)}, u32[]{:S(2)}) %collective-permute-start) | collective-permute-done | bytes 983072 | tf_op jit(solution)/shard_map/ppermute | solution.py:235
  131.0 21.3 %expert.3 = (bf16[640,768]{1,0:T(8,128)(2,1)}, bf16[640,768]{1,0:T(8,128)(2,1)}, bf16[640,3072]{1,0:T(8,128)(2,1)}, bf16[640,3072]{1,0:T(8,128)(2,1)}, bf16[640,768]{1,0:T(8,128)(2,1)}, /*index=5*/f32[128,768]{1,0:T(8,128)}) custom-call(bf16[640,768]{1,0:T(8,128)(2,1)} %collective-permute-done.x_ref.refs_1_, bf16[640,768]{1,0:T(8,128)(2,1)} %collective-permute-done.1.g_ref, ...), custom_call_target="tpu_custom_call" | custom-call | flops 12079595520 | bytes 17301504 | tf_op jit(solution)/shard_map/expert/pallas_call | solution.py:163
  152.3 0.7 collective-permute-start.2
  153.0 21.4 %expert.2 = (bf16[640,768]{1,0:T(8,128)(2,1)}, bf16[640,768]{1,0:T(8,128)(2,1)}, bf16[640,3072]{1,0:T(8,128)(2,1)}, bf16[640,3072]{1,0:T(8,128)(2,1)}, bf16[640,768]{1,0:T(8,128)(2,1)}, /*index=5*/f32[128,768]{1,0:T(8,128)}) custom-call(bf16[640,768]{1,0:T(8,128)(2,1)} %fusion.33.x_ref.refs_0_, bf16[640,768]{1,0:T(8,128)(2,1)} %fusion.36.g_ref, ...), custom_call_target="tpu_custom_call" | custom-call | flops 12079595520 | bytes 17301504 | tf_op jit(solution)/shard_map/expert/pallas_call | solution.py:163
  174.4 0.8 fusion.62
  175.3 4.3 multiply_reduce_fusion
  179.7 0.8 subtract_add_fusion
  180.9 2.6 convolution_convert_fusion.2.do_ref
  183.6 33.7 %attn_bwd.1 = (bf16[1024,768]{1,0:T(8,128)(2,1)}, bf16[1024,768]{1,0:T(8,128)(2,1)}, bf16[1024,768]{1,0:T(8,128)(2,1)}, f32[6,2,2048]{2,1,0:T(2,128)}) custom-call(bf16[1024,2304]{1,0:T(8,128)(2,1)} %convolution_convert_fusion.q_ref.k_ref.v_ref, bf16[1024,2304]{1,0:T(8,128)(2,1)} %convolution_convert_fusion.q_ref.k_ref.v_ref, ...), custom_call_target="tpu_custom_call" | custom-call | tf_op jit(solution)/shard_map/attn_bwd/pallas_call | solution.py:107
  217.3 1.7 constant_dynamic-update-slice_fusion.2
  219.7 1.6 copy-done.10
  221.3 6.4 %fusion.11 = (f32[768]{0:T(1024)S(1)}, f32[1024]{0:T(1024)}, f32[1024,768]{0,1:T(8,128)}) fusion(bf16[1024,768]{0,1:T(8,128)(2,1)S(1)} %copy.76, f32[1024]{0:T(1024)S(1)} %copy-done.19, f32[768]{0:T(1024)S(1)} %copy-done.15, bf16[1024,2304]{1,0:T(8,128)(2,1)S(1)} %constant_dynamic-update-slice_fusion, bf16[768,2432]{1,0:T(8,128)(2,1)S(1)} %copy-done.10), kind=kOutput, calls=%fused_computation.21 | convolution fusion | flops 3629381888 | bytes 12991488 | tf_op jit(solution)/shard_map/dot_general | solution.py:13
  227.7 0.6 broadcast_in_dim.65
  229.5 0.7 reshape.140
  230.2 0.8 broadcast_in_dim.67
  230.9 2.6 concatenate.23
  233.6 0.9 copy.96
  234.6 4.3 convolution_convert_fusion.3
  239.0 7.9 %convolution_convert_fusion.1 = bf16[768,2304]{1,0:T(8,128)(2,1)} fusion(bf16[1024,2304]{1,0:T(8,128)(2,1)} %copy-done.9, bf16[1024,768]{0,1:T(8,128)(2,1)S(1)} %copy.76, f32[768]{0:T(1024)S(1)} %copy-done.16, f32[1024]{0:T(1024)S(1)} %copy-done.20), kind=kOutput, calls=%fused_computation.11 | convolution fusion | flops 3628793856 | bytes 9837568 | tf_op jit(solution)/shard_map/dot_general | solution.py:372
  247.0 20.7 %expert_weights.1 = (bf16[768,3072]{1,0:T(8,128)(2,1)}, bf16[3072,768]{1,0:T(8,128)(2,1)}) custom-call(bf16[640,768]{1,0:T(8,128)(2,1)} %fusion.33.x_ref.refs_0_, bf16[640,768]{1,0:T(8,128)(2,1)} %collective-permute-done.x_ref.refs_1_, bf16[640,768]{1,0:T(8,128)(2,1)} %get-tuple-element.50.refs_2_, bf16[640,768]{1,0:T(8,128)(2,1)} %get-tuple-element.51.refs_3_, ...), custom_call_target="tpu_custom_call" | custom-call | flops 12079595520 | bytes 25165824 | tf_op jit(solution)/shard_map/expert_weights/pallas_call | solution.py:197
  267.8 1.4 collective-permute-start.3
  269.1 3.6 fusion.8
  272.8 1.6 copy.91
  274.4 0.9 copy.97
  275.3 16.0 %psum.35 = f32[96,128]{0,1:T(8,128)S(1)} all-reduce(f32[96,128]{0,1:T(8,128)S(1)} %copy.97), channel_id=1, replica_groups=mesh['rep'=4,'fsdp'=4,'expert'=2] {'rep'}, use_global_device_ids=true, to_apply=%region_10.11 | all-reduce | flops 12288 | bytes 98304 | tf_op jit(solution)/shard_map/psum | solution.py:395
  291.3 17.5 %reduce-scatter.8.cloned.1.call-done = bf16[96,768]{1,0:T(8,128)(2,1)} async-done(((bf16[768,768]{1,0:T(8,128)(2,1)}), bf16[96,768]{1,0:T(8,128)(2,1)}) %reduce-scatter.8.cloned.1.call-update) | async-done | bytes 147472 | tf_op jit(solution)/shard_map/reduce_scatter | solution.py:379
  308.8 51.8 %reduce-scatter.6.cloned.1.call-done = bf16[96,2304]{1,0:T(8,128)(2,1)} async-done(((bf16[768,2304]{1,0:T(8,128)(2,1)}), bf16[96,2304]{1,0:T(8,128)(2,1)}) %reduce-scatter.6.cloned.1.call-update) | async-done | bytes 442384 | tf_op jit(solution)/shard_map/reduce_scatter | solution.py:380
  361.8 0.7 copy.92
  362.5 5.0 add_convert_fusion
  367.5 1.6 copy.90
  369.1 181.4 %all-reduce.8.cloned.1.call-done = (bf16[1,768,3072]{2,1,0:T(8,128)(2,1)}, bf16[1,3072,768]{2,1,0:T(8,128)(2,1)}) async-done(((bf16[1,768,3072]{2,1,0:T(8,128)(2,1)}, bf16[1,3072,768]{2,1,0:T(8,128)(2,1)}), (bf16[1,768,3072]{2,1,0:T(8,128)(2,1)}, bf16[1,3072,768]{2,1,0:T(8,128)(2,1)})) %all-reduce.8.cloned.1.call-update) | async-done | bytes 9437200 | tf_op jit(solution)/shard_map/psum | solution.py:350
  550.5 7.5 %broadcast_in_dim.69 = f32[1,768,3072]{2,1,0:T(8,128)} convert(bf16[1,768,3072]{2,1,0:T(8,128)(2,1)} %get-tuple-element.112) | non-fusion elementwise | flops 2359296 | bytes 14155776 | tf_op jit(solution)/shard_map/broadcast_in_dim | solution.py:408
  558.0 4.5 broadcast_in_dim.71
  562.5 29.6 %all-reduce.10.cloned.1.call-done = (bf16[96,2304]{1,0:T(8,128)(2,1)}, bf16[96,768]{1,0:T(8,128)(2,1)}) async-done(((bf16[96,2304]{1,0:T(8,128)(2,1)}, bf16[96,768]{1,0:T(8,128)(2,1)}), (bf16[96,2304]{1,0:T(8,128)(2,1)}, bf16[96,768]{1,0:T(8,128)(2,1)})) %all-reduce.10.cloned.1.call-update) | async-done | bytes 589840 | tf_op jit(solution)/shard_map/psum | solution.py:395
  592.0 2.0 fusion.70
  594.0 1.6 convert_element_type.131
  (101 shorter events, 5.9 us)
Async XLA Ops:
  7.2 6.8 %copy-start.12 = (s32[1024,1]{0,1:T(1,128)S(1)}, s32[1024,1]{0,1:T(1,128)}, u32[]{:S(2)}) copy-start(s32[1024,1]{0,1:T(1,128)} %param.19) | copy-start | bytes 12292
  7.2 41.1 %all-gather.3.cloned.1.call-start = ((), (), s32[]{:S(2)}) async-start(), calls=%async_computation.3 | async-start | bytes 4202496 | tf_op jit(solution)/shard_map/all_gather | solution.py:287
  12.2 90.0 %all-gather.5.cloned.1.call-start = ((), (), s32[]{:S(2)}) async-start(), calls=%async_computation.4 | async-start | bytes 1327104 | tf_op jit(solution)/shard_map/all_gather | solution.py:295
  12.3 4.5 copy-start.24
  14.0 3.9 copy-start.26
  14.0 3.9 copy-start.13
  17.9 40.4 %copy-start.18 = (f32[1024]{0:T(1024)}, f32[1024]{0:T(1024)S(1)}, u32[]{:S(2)}) copy-start(f32[1024]{0:T(1024)S(1)} %get-tuple-element.122) | copy-start | bytes 12292
  17.9 157.4 %copy-start.21 = (s32[1024]{0:T(1024)}, s32[1024]{0:T(1024)S(1)}, u32[]{:S(2)}) copy-start(s32[1024]{0:T(1024)S(1)} %fusion.66) | copy-start | bytes 12292
  48.3 226.0 %reduce-scatter.10.cloned.1.call-start = ((), (), s32[]{:S(2)}) async-start(), calls=%async_computation.7 | async-start | bytes 442368
  49.4 4.0 copy-start.7
  55.5 59.9 %collective-permute-start.1 = (bf16[640,768]{1,0:T(8,128)(2,1)}, bf16[640,768]{1,0:T(8,128)(2,1)}, u32[]{:S(2)}, u32[]{:S(2)}) collective-permute-start(bf16[640,768]{1,0:T(8,128)(2,1)} %fusion.42), channel_id=1, source_target_pairs={{0,1},{1,0},{2,3},{3,2},{4,5},{5,4},{6,7},{7,6},{8,9},{9,8},{10,11... | collective-permute-start | bytes 2949128 | tf_op jit(solution)/shard_map/ppermute | solution.py:235
  58.3 7.8 %copy-start.14 = (f32[768]{0:T(1024)}, f32[768]{0:T(1024)S(1)}, u32[]{:S(2)}) copy-start(f32[768]{0:T(1024)S(1)} %get-tuple-element.111) | copy-start | bytes 9220
  102.2 3.5 copy-start.8
  105.7 74.0 %copy-start.2 = (f32[1024,768]{0,1:T(8,128)}, f32[1024,768]{0,1:T(8,128)S(1)}, u32[]{:S(2)}) copy-start(f32[1024,768]{0,1:T(8,128)S(1)} %get-tuple-element.126) | copy-start | bytes 9437188
  105.7 3.3 copy-start.3
  107.2 23.8 %collective-permute-start = (bf16[640,768]{1,0:T(8,128)(2,1)S(1)}, bf16[640,768]{1,0:T(8,128)(2,1)}, u32[]{:S(2)}, u32[]{:S(2)}) collective-permute-start(bf16[640,768]{1,0:T(8,128)(2,1)S(1)} %fusion.39), channel_id=1, source_target_pairs={{0,1},{1,0},{2,3},{3,2},{4,5},{5,4},{6,7},{7,6},{8,9},{9,8},{10,11... | collective-permute-start | bytes 2949128 | tf_op jit(solution)/shard_map/ppermute | solution.py:235
  152.3 23.1 %collective-permute-start.2 = (bf16[640,768]{1,0:T(8,128)(2,1)}, bf16[640,768]{1,0:T(8,128)(2,1)S(1)}, u32[]{:S(2)}, u32[]{:S(2)}) collective-permute-start(bf16[640,768]{1,0:T(8,128)(2,1)} %get-tuple-element.40), channel_id=1, source_target_pairs={{0,1},{1,0},{2,3},{3,2},{4,5},{5,4},{6,7},{7,6},{8,9},{9,8},{10,11... | collective-permute-start | bytes 2949128 | tf_op jit(solution)/shard_map/ppermute | solution.py:235
  179.7 1.3 copy-start.27
  180.9 2.6 copy-start
  217.2 1.9 copy-start.5
  217.3 2.3 copy-start.4
  219.1 2.2 copy-start.10
  219.1 2.2 copy-start.15
  219.1 2.2 copy-start.19
  221.3 6.4 %copy-start.9 = (bf16[1024,2304]{1,0:T(8,128)(2,1)}, bf16[1024,2304]{1,0:T(8,128)(2,1)S(1)}, u32[]{:S(2)}) copy-start(bf16[1024,2304]{1,0:T(8,128)(2,1)S(1)} %constant_dynamic-update-slice_fusion) | copy-start | bytes 14155780
  221.3 7.6 %copy-start.11 = (f32[6,2,2048]{2,1,0:T(2,128)S(1)}, f32[6,2,2048]{2,1,0:T(2,128)}, u32[]{:S(2)}) copy-start(f32[6,2,2048]{2,1,0:T(2,128)} %get-tuple-element.49) | copy-start | bytes 294916
  221.3 7.7 %copy-start.23 = (s32[8,4]{0,1:T(4,128)S(1)}, s32[8,4]{0,1:T(4,128)}, u32[]{:S(2)}) copy-start(s32[8,4]{0,1:T(4,128)} %multiply_add_fusion) | copy-start | bytes 388
  221.3 13.2 %copy-start.6 = (bf16[1024,768]{1,0:T(8,128)(2,1)S(1)}, bf16[1024,768]{1,0:T(8,128)(2,1)}, u32[]{:S(2)}) copy-start(bf16[1024,768]{1,0:T(8,128)(2,1)} %get-tuple-element.35.o_ref) | copy-start | bytes 4718596
  234.5 4.5 copy-start.16
  234.5 4.5 copy-start.20
  234.5 74.3 %reduce-scatter.8.cloned.1.call-start = ((), (), s32[]{:S(2)}) async-start(), calls=%async_computation.6 | async-start | bytes 1327104 | tf_op jit(solution)/shard_map/reduce_scatter | solution.py:379
  238.9 121.7 %reduce-scatter.6.cloned.1.call-start = ((), (), s32[]{:S(2)}) async-start(), calls=%async_computation.5 | async-start | bytes 3981312 | tf_op jit(solution)/shard_map/reduce_scatter | solution.py:380
  247.0 303.5 %all-reduce.8.cloned.1.call-start = ((), (), s32[]{:S(2)}) async-start(), calls=%async_computation.8 | async-start | bytes 18874368 | tf_op jit(solution)/shard_map/psum | solution.py:350
  267.7 1.5 copy-start.25
  267.7 1.5 copy-start.17
  267.7 324.3 %all-reduce.10.cloned.1.call-start = ((), (), s32[]{:S(2)}) async-start(), calls=%async_computation.9 | async-start | bytes 1179648 | tf_op jit(solution)/shard_map/psum | solution.py:395
  267.8 94.7 %collective-permute-start.3 = (bf16[640,768]{1,0:T(8,128)(2,1)}, bf16[640,768]{1,0:T(8,128)(2,1)}, u32[]{:S(2)}, u32[]{:S(2)}) collective-permute-start(bf16[640,768]{1,0:T(8,128)(2,1)} %get-tuple-element.41), channel_id=1, source_target_pairs={{0,1},{1,0},{2,3},{3,2},{4,5},{5,4},{6,7},{7,6},{8,9},{9,8},{10,11... | collective-permute-start | bytes 2949128 | tf_op jit(solution)/shard_map/ppermute | solution.py:235
  272.8 89.7 %copy-start.22 = (s32[1024]{0:T(1024)S(1)}, s32[1024]{0:T(1024)}, u32[]{:S(2)}) copy-start(s32[1024]{0:T(1024)} %copy-done.21) | copy-start | bytes 12292
  550.5 7.5 %copy-start.1 = (bf16[1,3072,768]{2,1,0:T(8,128)(2,1)S(1)}, bf16[1,3072,768]{2,1,0:T(8,128)(2,1)}, u32[]{:S(2)}) copy-start(bf16[1,3072,768]{2,1,0:T(8,128)(2,1)} %get-tuple-element.113) | copy-start | bytes 14155780
Sparse Core Ops, SparseCore 0:
  12.3 35.9 all-gather.2
  50.2 28.7 all-gather.4
  234.6 33.7 reduce-scatter.9
  272.0 36.7 reduce-scatter.7
  312.6 48.0 reduce-scatter.5
  365.3 185.1 all-reduce.7
  552.9 39.1 all-reduce.9
where the time goes:
time: 614 us; the launch traced here: 603 us
  waiting for transfers between devices  325 us (53%)
  Pallas kernels  133 us (22%)
  matrix products  52.4 us (9%)
  local copies, waits for them, and re-layouts  31 us (5%)
  other arithmetic  26.1 us (4%)
  blocking collectives  16 us (3%)
  between operations  15.1 us (2%)
    psum x1, waiting for transfers between devices, body(): sum_in, sum_out = lax.psum((d_in, d_out), ('rep', 'fsdp'))  181 us
    reduce_scatter x1, waiting for transfers between devices, body(): share_in = lax.psum_scatter(d_proj, GROUP, scatter_dimension=0, tiled=True)  51.8 us
    pallas_call x2, Pallas kernels, expert(): pl.pallas_call(functools.partial(expert_kernel, experts), grid=(ff // FB,...  42.7 us
    pallas_call x1, Pallas kernels, attn_fwd(): pl.pallas_call(functools.partial(attn_fwd_kernel, head ** (-0.5), head),...  36.1 us
    pallas_call x1, Pallas kernels, attn_bwd(): pl.pallas_call(functools.partial(attn_bwd_kernel, head ** (-0.5), head),...  33.7 us
    dot_general x9, matrix products, dot32(): return jnp.dot(left, right, preferred_element_type=F32)  30.8 us
    psum x1, waiting for transfers between devices, body(): lax.psum((share_out, share_in, share_small), 'rep')  29.6 us
    all_gather x1, waiting for transfers between devices, body(): gathered = lax.all_gather(packed, GROUP, axis=0, tiled=True)  28.6 us
  transfers between devices with their start and end apart: 11, of which 7 were waited for; matrix products, arithmetic and copies ran while one was open for 13% of the time, Pallas kernels for 13%

commit v1 on v0

v1 whole, which is shorter than its diff:
```python
import functools

import jax
import jax.numpy as jnp
from jax import lax
from jax.experimental import pallas as pl
from jax.experimental.pallas import tpu as pltpu
from jax.sharding import PartitionSpec as P

F32 = jnp.float32
BF = jnp.bfloat16
ROWS = 512
TILE = 128
VMEM_BYTES = 56 * 2**20


def dot_t(a, b):
    return lax.dot_general(a, b, (((1,), (1,)), ((), ())), preferred_element_type=F32)


def dot_n(a, b):
    return lax.dot_general(a, b, (((1,), (0,)), ((), ())), preferred_element_type=F32)


def skew(row, wide, out_ref):
    x = pltpu.roll(jnp.broadcast_to(row, (8, wide)), wide - (TILE - 1), 1)
    index = lax.broadcasted_iota(jnp.int32, x.shape, 0)
    for bit in (1, 2, 4):
        x = jnp.where((index & bit) != 0, pltpu.roll(x, bit, 1), x)
    n = 8
    while n < TILE:
        x = jnp.concatenate([x, pltpu.roll(x, n, 1)], axis=0)
        n *= 2
    out_ref[...] = x


def unskew(x, wide):
    n = x.shape[0]
    while n > 8:
        n //= 2
        x = x[:n] + pltpu.roll(x[n:], wide - n, 1)
    index = lax.broadcasted_iota(jnp.int32, x.shape, 0)
    for bit in (4, 2, 1):
        x = jnp.where((index & bit) != 0, pltpu.roll(x, wide - bit, 1), x)
    total = jnp.broadcast_to(jnp.sum(x, axis=0, keepdims=True), (8, wide))
    return pltpu.roll(total, TILE - 1, 1)[:1]


def attn_fwd_kernel(
    scaling, head, q_ref, k_ref, v_ref, sq_ref, sk_ref, off_ref, o_ref, inv_ref, e_ref, bias0, bias1
):
    length = q_ref.shape[0]
    wide = off_ref.shape[-1]
    lane = lax.broadcasted_iota(jnp.int32, (1, 2 * head), 1)
    firsts = lane < head
    bias = (bias0, bias1)
    for hh in range(2):
        skew(off_ref[0, hh : hh + 1, :], wide, bias[hh])
    kx = jnp.concatenate([k_ref[...], sk_ref[...]], axis=1)
    vx = v_ref[...]
    for b in range(length // ROWS):
        rows = pl.ds(b * ROWS, ROWS)
        q = q_ref[rows, :].astype(F32) * scaling
        made = []
        for hh in range(2):
            mine = firsts if hh == 0 else jnp.logical_not(firsts)
            qx = jnp.concatenate([jnp.where(mine, q, 0.0).astype(BF), sq_ref[rows, :]], axis=1)
            tiles = []
            for a in range(ROWS // TILE):
                at = length - TILE * (1 + a) - b * ROWS
                tiles.append(bias[hh][:, at : at + length])
            s = dot_t(qx, kx) + jnp.concatenate(tiles, axis=0)
            e = jnp.exp(s - jnp.max(s, axis=-1, keepdims=True)).astype(BF)
            e_ref[0, hh, rows, :] = e
            made.append(dot_n(e, jnp.where(mine, vx, jnp.ones_like(vx))))
        sums = jnp.where(firsts, pltpu.roll(made[0], head, 1), pltpu.roll(made[1], head, 1))
        inv = 1.0 / sums
        inv_ref[rows, :] = inv
        o_ref[rows, :] = (jnp.where(firsts, made[0], made[1]) * inv).astype(BF)


def attn_fwd(qkv, sq, sk, off, heads, head):
    length = qkv.shape[0]
    pairs = heads // 2
    wide = off.shape[-1]
    col = lambda at: pl.BlockSpec((length, 2 * head), lambda p: (0, at + p))
    fixed = pl.BlockSpec((length, 128), lambda p: (0, 0))
    return pl.pallas_call(
        functools.partial(attn_fwd_kernel, head**-0.5, head),
        grid=(pairs,),
        in_specs=[
            col(0), col(pairs), col(2 * pairs), fixed, fixed,
            pl.BlockSpec((1, 2, wide), lambda p: (p, 0, 0)),
        ],
        out_specs=[col(0), col(0), pl.BlockSpec((1, 2, length, length), lambda p: (p, 0, 0, 0))],
        out_shape=[
            jax.ShapeDtypeStruct((length, heads * head), BF),
            jax.ShapeDtypeStruct((length, heads * head), F32),
            jax.ShapeDtypeStruct((pairs, 2, length, length), BF),
        ],
        scratch_shapes=[pltpu.VMEM((TILE, wide), F32)] * 2,
        compiler_params=pltpu.CompilerParams(vmem_limit_bytes=VMEM_BYTES),
        cost_estimate=pl.CostEstimate(
            flops=40 * heads * length * length * head // 2,
            bytes_accessed=2 * heads * length * length,
            transcendentals=heads * length * length,
        ),
        name="attn_fwd",
    )(qkv, qkv, qkv, sq, sk, off)


def attn_bwd_kernel(
    scaling, head, q_ref, k_ref, v_ref, do_ref, o_ref, inv_ref, e_ref,
    dq_ref, dk_ref, dv_ref, doff_ref, acc0, acc1, dkt, dvt,
):
    length = q_ref.shape[0]
    wide = acc0.shape[-1]
    lane = lax.broadcasted_iota(jnp.int32, (1, 2 * head), 1)
    firsts = lane < head
    acc = (acc0, acc1)
    for ref in (acc0, acc1, dkt, dvt):
        ref[...] = jnp.zeros_like(ref)
    lane_b = lax.broadcasted_iota(jnp.int32, (ROWS, 128), 1)
    extra = jnp.where(lax.broadcasted_iota(jnp.int32, (length, 128), 1) < 2, 1.0, 0.0).astype(BF)
    vx = jnp.concatenate([v_ref[...], extra], axis=1)
    kx = k_ref[...]
    for b in range(length // ROWS):
        rows = pl.ds(b * ROWS, ROWS)
        do = do_ref[rows, :].astype(F32) * inv_ref[rows, :]
        toward = do * o_ref[rows, :].astype(F32)
        qt = q_ref[rows, :].T
        dot = do.astype(BF).T
        made = []
        for hh in range(2):
            mine = firsts if hh == 0 else jnp.logical_not(firsts)
            part = slice(hh * head, (hh + 1) * head)
            delta = -jnp.sum(jnp.where(mine, toward, 0.0), axis=-1, keepdims=True)
            hi = delta.astype(BF).astype(F32)
            ext = jnp.where(lane_b == 0, hi, jnp.where(lane_b == 1, delta - hi, 0.0)).astype(BF)
            dp = dot_t(jnp.concatenate([jnp.where(mine, do, 0.0).astype(BF), ext], axis=1), vx)
            e = e_ref[0, hh, rows, :]
            ds = e.astype(F32) * dp
            for a in range(ROWS // TILE):
                at = length - TILE * (1 + a) - b * ROWS
                acc[hh][:, at : at + length] += ds[a * TILE : (a + 1) * TILE]
            low = ds.astype(BF)
            made.append(dot_n(low, kx))
            dkt[part, :] += dot_n(qt[part], low)
            dvt[part, :] += dot_n(dot[part], e)
        dq_ref[rows, :] = (jnp.where(firsts, made[0], made[1]) * scaling).astype(BF)
    for hh in range(2):
        doff_ref[0, hh : hh + 1, :] = unskew(acc[hh][...], wide)
    dk_ref[...] = (dkt[...].T * scaling).astype(BF)
    dv_ref[...] = dvt[...].T.astype(BF)


def attn_bwd(qkv, do, o, inv, e, wide, heads, head):
    length = qkv.shape[0]
    pairs = heads // 2
    col = lambda at: pl.BlockSpec((length, 2 * head), lambda p: (0, at + p))
    return pl.pallas_call(
        functools.partial(attn_bwd_kernel, head**-0.5, head),
        grid=(pairs,),
        in_specs=[
            col(0), col(pairs), col(2 * pairs), col(0), col(0), col(0),
            pl.BlockSpec((1, 2, length, length), lambda p: (p, 0, 0, 0)),
        ],
        out_specs=[col(0), col(0), col(0), pl.BlockSpec((1, 2, wide), lambda p: (p, 0, 0))],
        out_shape=[jax.ShapeDtypeStruct((length, heads * head), BF)] * 3
        + [jax.ShapeDtypeStruct((pairs, 2, wide), F32)],
        scratch_shapes=[pltpu.VMEM((TILE, wide), F32)] * 2
        + [pltpu.VMEM((2 * head, length), F32)] * 2,
        compiler_params=pltpu.CompilerParams(vmem_limit_bytes=VMEM_BYTES),
        cost_estimate=pl.CostEstimate(
            flops=40 * heads * length * length * head // 2,
            bytes_accessed=2 * heads * length * length,
            transcendentals=0,
        ),
        name="attn_bwd",
    )(qkv, qkv, qkv, do, o, inv, e)
FF_BLOCK = 512


def gelu_pair(u):
    c = 0.7978845608028654
    sq = u * u
    t = jnp.tanh(u * (c + (0.044715 * c) * sq))
    half = 0.5 + 0.5 * t
    return u * half, half + (0.5 * u) * (1.0 - t * t) * (c + (3.0 * 0.044715 * c) * sq)


def probabilities(x, router, experts):
    logits = dot_n(x, router)
    lane = lax.broadcasted_iota(jnp.int32, logits.shape, 1)
    logits = jnp.where(lane < experts, logits, -1e30)
    e = jnp.exp(logits - jnp.max(logits, axis=-1, keepdims=True))
    return e / jnp.sum(e, axis=-1, keepdims=True)


def hidden_step(x_ref, deo_ref, win_ref, wout_ref, act_ref, du_ref):
    win, wout = win_ref[0], wout_ref[0]
    rows = x_ref.shape[0]
    parts = 2 if rows % 32 == 0 else 1
    step = rows // parts
    for at in range(0, rows, step):
        part = pl.ds(at, step)
        u = dot_n(x_ref[part, :], win)
        dact = dot_t(deo_ref[part, :], wout)
        a, slope = gelu_pair(u)
        act_ref[part, :] = a.astype(BF)
        du_ref[part, :] = (dact * slope).astype(BF)


def gated_cotangent(experts, x_ref, g_ref, router_ref, mine_ref, deo_ref):
    probs = probabilities(x_ref[...], router_ref[...], experts)
    gate = jnp.sum(probs * mine_ref[...], axis=-1, keepdims=True)
    deo_ref[...] = (gate * g_ref[...].astype(F32)).astype(BF)


def hidden_kernel(
    experts, x_ref, g_ref, router_ref, mine_ref, win_ref, wout_ref, act_ref, du_ref, deo_ref
):
    @pl.when(pl.program_id(0) == 0)
    def _():
        gated_cotangent(experts, x_ref, g_ref, router_ref, mine_ref, deo_ref)

    hidden_step(x_ref, deo_ref, win_ref, wout_ref, act_ref, du_ref)


def fixed(*shape):
    return pl.BlockSpec(shape, lambda f: (0,) * len(shape))


def in_block(width):
    return pl.BlockSpec((1, width, FF_BLOCK), lambda f: (0, 0, f))


def out_block(width):
    return pl.BlockSpec((1, FF_BLOCK, width), lambda f: (0, f, 0))


def slot_block(rows):
    return pl.BlockSpec((rows, FF_BLOCK), lambda f: (0, f))


def expert_hidden(x, g, router, mine, win, wout, experts):
    rows, width = x.shape
    ff = win.shape[-1]
    return pl.pallas_call(
        functools.partial(hidden_kernel, experts),
        grid=(ff // FF_BLOCK,),
        in_specs=[
            fixed(rows, width), fixed(rows, width), fixed(width, 128), fixed(1, 128),
            in_block(width), out_block(width),
        ],
        out_specs=[slot_block(rows), slot_block(rows), fixed(rows, width)],
        out_shape=[
            jax.ShapeDtypeStruct((rows, ff), BF),
            jax.ShapeDtypeStruct((rows, ff), BF),
            jax.ShapeDtypeStruct((rows, width), BF),
        ],
        compiler_params=pltpu.CompilerParams(vmem_limit_bytes=VMEM_BYTES),
        cost_estimate=pl.CostEstimate(
            flops=8 * rows * width * ff,
            bytes_accessed=4 * width * ff + 4 * rows * ff,
            transcendentals=rows * ff,
        ),
        name="expert_hidden",
    )(x, g, router, mine, win, wout)


def gradients_kernel(
    experts, x_ref, g_ref, router_ref, mine_ref, win_ref, wout_ref, xl_ref, deol_ref, actl_ref,
    dul_ref, act_ref, du_ref, deo_ref, din_ref, dout_ref, xt, xlt,
):
    @pl.when(pl.program_id(0) == 0)
    def _():
        gated_cotangent(experts, x_ref, g_ref, router_ref, mine_ref, deo_ref)
        xt[...] = x_ref[...].T
        xlt[...] = xl_ref[...].T

    hidden_step(x_ref, deo_ref, win_ref, wout_ref, act_ref, du_ref)
    din_ref[...] = (dot_n(xlt[...], dul_ref[...]) + dot_n(xt[...], du_ref[...])).astype(BF)
    dout_ref[...] = (dot_n(actl_ref[...].T, deol_ref[...]) + dot_n(act_ref[...].T, deo_ref[...])).astype(BF)


def expert_gradients(x, g, router, mine, win, wout, x_local, deo_local, act_local, du_local, experts):
    rows, width = x.shape
    own = x_local.shape[0]
    ff = win.shape[-1]
    return pl.pallas_call(
        functools.partial(gradients_kernel, experts),
        grid=(ff // FF_BLOCK,),
        in_specs=[
            fixed(rows, width), fixed(rows, width), fixed(width, 128), fixed(1, 128),
            in_block(width), out_block(width), fixed(own, width), fixed(own, width),
            slot_block(own), slot_block(own),
        ],
        out_specs=[
            slot_block(rows), slot_block(rows), fixed(rows, width),
            pl.BlockSpec((width, FF_BLOCK), lambda f: (0, f)),
            pl.BlockSpec((FF_BLOCK, width), lambda f: (f, 0)),
        ],
        out_shape=[
            jax.ShapeDtypeStruct((rows, ff), BF),
            jax.ShapeDtypeStruct((rows, ff), BF),
            jax.ShapeDtypeStruct((rows, width), BF),
            jax.ShapeDtypeStruct((width, ff), BF),
            jax.ShapeDtypeStruct((ff, width), BF),
        ],
        scratch_shapes=[pltpu.VMEM((width, rows), BF), pltpu.VMEM((width, own), BF)],
        compiler_params=pltpu.CompilerParams(vmem_limit_bytes=VMEM_BYTES),
        cost_estimate=pl.CostEstimate(
            flops=12 * (rows + own) * width * ff,
            bytes_accessed=8 * width * ff + 4 * (rows + own) * ff,
            transcendentals=rows * ff,
        ),
        name="expert_gradients",
    )(x, g, router, mine, win, wout, x_local, deo_local, act_local, du_local)


def results_kernel(
    experts, x_ref, g_ref, router_ref, mine_ref, win_ref, wout_ref, act_ref, du_ref,
    geo_ref, dn_ref, drouter_ref, eo, dx,
):
    step = pl.program_id(0)

    @pl.when(step == 0)
    def _():
        eo[...] = dot_n(act_ref[...], wout_ref[0])
        dx[...] = dot_t(du_ref[...], win_ref[0])

    @pl.when(step > 0)
    def _():
        eo[...] += dot_n(act_ref[...], wout_ref[0])
        dx[...] += dot_t(du_ref[...], win_ref[0])

    @pl.when(step == pl.num_programs(0) - 1)
    def _():
        made = eo[...].astype(BF).astype(F32)
        mine = mine_ref[...]
        probs = probabilities(x_ref[...], router_ref[...], experts)
        gate = jnp.sum(probs * mine, axis=-1, keepdims=True)
        geo_ref[...] = (gate * made).astype(BF)
        dgate = jnp.sum(made * g_ref[...].astype(F32), axis=-1, keepdims=True)
        dprobs = mine * dgate
        dlog = probs * (dprobs - jnp.sum(probs * dprobs, axis=-1, keepdims=True))
        dlog = dlog.astype(BF)
        dn_ref[...] = (dx[...] + dot_t(dlog, router_ref[...])).astype(BF)
        drouter_ref[...] = dot_n(dlog.T, x_ref[...])


def expert_results(x, g, router, mine, win, wout, act, du, experts):
    rows, width = x.shape
    ff = win.shape[-1]
    return pl.pallas_call(
        functools.partial(results_kernel, experts),
        grid=(ff // FF_BLOCK,),
        in_specs=[
            fixed(rows, width), fixed(rows, width), fixed(width, 128), fixed(1, 128),
            in_block(width), out_block(width), slot_block(rows), slot_block(rows),
        ],
        out_specs=[fixed(rows, width), fixed(rows, width), fixed(128, width)],
        out_shape=[
            jax.ShapeDtypeStruct((rows, width), BF),
            jax.ShapeDtypeStruct((rows, width), BF),
            jax.ShapeDtypeStruct((128, width), F32),
        ],
        scratch_shapes=[pltpu.VMEM((rows, width), F32), pltpu.VMEM((rows, width), F32)],
        compiler_params=pltpu.CompilerParams(vmem_limit_bytes=VMEM_BYTES),
        cost_estimate=pl.CostEstimate(
            flops=8 * rows * width * ff,
            bytes_accessed=4 * width * ff + 4 * rows * ff,
            transcendentals=0,
        ),
        name="expert_results",
    )(x, g, router, mine, win, wout, act, du)
EPS = 1e-06
NEG = -1e30
HIGH = lax.Precision.HIGHEST
GROUP = ("fsdp", "expert")


def normalize(values, gain):
    row_scale = lax.rsqrt(jnp.mean(values * values, axis=-1, keepdims=True) + EPS)
    return (values * row_scale * gain, row_scale)


def normalize_back(values, row_scale, gain, cotangent):
    weighted = cotangent * gain
    d_gain = jnp.sum(cotangent * values * row_scale, axis=0)
    d_values = row_scale * weighted - values * row_scale**3 * jnp.mean(
        weighted * values, axis=-1, keepdims=True
    )
    return (d_values, d_gain)


def dot32(left, right):
    return jnp.dot(left, right, preferred_element_type=F32)


def bits_of(axis, size):
    return [(axis, size >> (k + 1)) for k in range(size.bit_length() - 1)]


def partner(value, key, sizes):
    axis, bit = key
    return lax.ppermute(value, axis, [(i, i ^ bit) for i in range(sizes[axis])])


def side(key):
    return lax.rem(lax.axis_index(key[0]) // key[1], 2)


def gather_bits(value, order, keys, sizes):
    held = []
    shape = value.shape
    for key in order:
        got = partner(value, key, sizes)
        at = sum(keys.index(other) < keys.index(key) for other in held)
        lower = side(key) == 0
        value = jnp.where(lower, jnp.stack([value, got], at), jnp.stack([got, value], at))
        held.append(key)
    return value.reshape((-1,) + shape[1:])


def scatter_bits(value, order, keys, sizes):
    held = list(keys)
    value = value.reshape((2,) * len(keys) + (value.shape[0] >> len(keys),) + value.shape[1:])
    for key in order:
        at = held.index(key)
        mine = side(key)
        got = partner(lax.dynamic_index_in_dim(value, 1 - mine, at, False), key, sizes)
        kept = lax.dynamic_index_in_dim(value, mine, at, False)
        value = (kept.astype(F32) + got.astype(F32)).astype(value.dtype)
        held.remove(key)
    return value


def shift(value, axis, by, size):
    return lax.ppermute(value, axis, [(i, (i + by) % size) for i in range(size)])


def sum_over(value, axis, size):
    me = lax.axis_index(axis)
    blocks = value.reshape((size, value.shape[0] // size) + value.shape[1:])
    total = lax.dynamic_index_in_dim(blocks, me, 0, False).astype(F32)
    for s in range(1, size):
        block = lax.dynamic_index_in_dim(blocks, lax.rem(me + s, size), 0, False)
        total = total + shift(block, axis, s, size).astype(F32)
    total = total.astype(value.dtype)
    out = lax.dynamic_update_index_in_dim(jnp.zeros_like(blocks), total, me, 0)
    for s in range(1, size):
        got = shift(total, axis, s, size)
        out = lax.dynamic_update_index_in_dim(out, got, lax.rem(me - s + size, size), 0)
    return out.reshape(value.shape)


def swap(blocks, sign, experts):
    moved = [
        lax.ppermute(block, "expert", [(i, (i + sign * (at + 1)) % experts) for i in range(experts)])
        for at, block in enumerate(blocks)
    ]
    return moved


def after(value, earlier):
    return lax.optimization_barrier((value, earlier))[0]


def body(
    sizes,
    tokens,
    segment_ids,
    offset_bucket,
    routes,
    capacity_keep,
    gain_attn,
    gain_ffn,
    w_query,
    w_key,
    w_value,
    w_output,
    rel_table,
    router,
    expert_in,
    expert_out,
    grad_out,
):
    length = segment_ids.shape[1]
    heads = rel_table.shape[1]
    inner = w_query.shape[1]
    head = inner // heads
    experts = router.shape[1]
    token_rows, width = tokens.shape
    capacity = token_rows * 5 // (4 * experts)
    slots = experts * capacity
    shard = w_query.shape[0]
    group_size = sizes["fsdp"] * sizes["expert"]
    own_buckets = rel_table.shape[0]
    buckets = own_buckets * group_size
    me = lax.axis_index("expert")
    ways, others = bits_of("fsdp", sizes["fsdp"]), bits_of("expert", sizes["expert"])
    keys = ways + others

    small_cols = [
        gain_attn[:, None],
        gain_ffn[:, None],
        router,
        jnp.pad(rel_table, ((0, shard - own_buckets), (0, 0))),
    ]
    used = 2 + experts + heads
    packed = jnp.concatenate(
        [w_query, w_key, w_value] + small_cols + [jnp.zeros((shard, -used % 128), BF)], axis=1
    )
    half = packed.shape[1] // 256 * 128
    gathered = jnp.concatenate(
        [
            gather_bits(packed[:, :half], others + ways, keys, sizes),
            gather_bits(packed[:, half:], ways[:-1] + others + ways[-1:], keys, sizes),
        ],
        axis=1,
    )
    proj_in = gathered[:, : 3 * inner]
    small = gathered[:, 3 * inner :]
    gain_one = small[:, 0].astype(F32)
    gain_two = small[:, 1].astype(F32)
    route_weight = small[:, 2 : 2 + experts]
    table = small[:, 2 + experts : used].reshape(group_size, shard, heads)[:, :own_buckets]
    table = table.reshape(buckets, heads)
    proj_output = lax.all_gather(after(w_output, gathered), GROUP, axis=0, tiled=True)

    chosen = routes[:, 0]
    picked = (chosen[:, None] == jnp.arange(experts, dtype=jnp.int32)[None, :]).astype(jnp.int32)
    earlier = jnp.cumsum(picked, axis=0) - picked
    slot = lax.rem(chosen - me + experts, experts) * capacity + jnp.sum(earlier * picked, axis=-1)
    slot = jnp.where(capacity_keep == 1, slot, slots)
    slot_ids = jnp.arange(slots, dtype=jnp.int32)
    to_slots = (slot_ids[:, None] == slot[None, :]).astype(BF)
    to_tokens = (slot[:, None] == slot_ids[None, :]).astype(BF)

    def leave(values, first, last):
        return dot32(to_slots[first:last], values).astype(BF)

    def depart(values):
        return [leave(values, s * capacity, (s + 1) * capacity) for s in range(1, experts)]

    g_local = leave(grad_out, 0, capacity)
    g_remote = jnp.concatenate(
        swap([after(block, gathered) for block in depart(grad_out)], 1, experts), axis=0
    )

    inputs = tokens.astype(F32)
    normed, scale_one = normalize(inputs, gain_one)
    normed_low = normed.astype(BF)
    qkv = dot32(normed_low, proj_in).astype(BF)

    bucket_of = jnp.concatenate([offset_bucket, jnp.full((1,), -1, jnp.int32)])
    hits = (bucket_of[None, :] == jnp.arange(buckets, dtype=jnp.int32)[:, None]).astype(BF)
    offsets = dot32(table.T, hits).reshape(heads // 2, 2, 2 * length)
    same = segment_ids[0][:, None] == jnp.arange(128, dtype=jnp.int32)[None, :]
    seg_q = jnp.where(same, 0.0, NEG).astype(BF)
    seg_k = same.astype(BF)
    attn_out, inverse, weights = attn_fwd(qkv, seg_q, seg_k, offsets, heads, head)

    resid = inputs + dot32(attn_out, proj_output)
    normed_two, scale_two = normalize(resid, gain_two)
    second_low = normed_two.astype(BF)

    x_remote = jnp.concatenate(swap(depart(second_low), 1, experts), axis=0)
    x_local = leave(second_low, 0, capacity)
    route_wide = jnp.pad(route_weight, ((0, 0), (0, 128 - experts)))
    mine = (jnp.arange(128, dtype=jnp.int32) == me).astype(F32)[None, :]
    shared = (route_wide, mine, expert_in, expert_out)
    act_l, du_l, deo_l = expert_hidden(x_local, g_local, *shared, experts)
    act_r, du_r, deo_r, d_in, d_out = expert_gradients(
        x_remote, g_remote, *shared, x_local, deo_l, act_l, du_l, experts
    )
    sum_in, sum_out = lax.psum((d_in, d_out), ("rep", "fsdp"))

    def cut(rows):
        return [rows[s * capacity : (s + 1) * capacity] for s in range(experts - 1)]

    geo_r, dn_r, dr_r = expert_results(
        x_remote, g_remote, *shared, after(act_r, d_in), du_r, experts
    )
    dn_back = swap(cut(dn_r), -1, experts)
    geo_l, dn_l, dr_l = expert_results(
        x_local, g_local, *shared, after(act_l, dn_r), du_l, experts
    )
    d_second = dot32(to_tokens, jnp.concatenate([dn_l] + dn_back, axis=0))
    geo_back = swap(cut(after(geo_r, dn_back[-1])), -1, experts)
    output = resid + dot32(to_tokens, jnp.concatenate([geo_l] + geo_back, axis=0))
    output = output.astype(BF)
    d_router = (dr_l + dr_r)[:experts].T

    cotangent = grad_out.astype(F32)
    d_resid_norm, d_gain_two = normalize_back(resid, scale_two, gain_two, d_second)
    d_resid = cotangent + d_resid_norm
    d_branch = d_resid.astype(BF)
    d_attn = dot_t(d_branch, proj_output).astype(BF)
    d_proj_output = lax.dot_general(
        attn_out, d_branch, (((0,), (0,)), ((), ())), preferred_element_type=F32
    ).astype(BF)
    d_query, d_key, d_value, d_offsets = attn_bwd(
        qkv, d_attn, attn_out, inverse, weights, 2 * length, heads, head
    )
    d_table = jnp.dot(
        hits.astype(F32), d_offsets.reshape(heads, 2 * length).T, precision=HIGH
    )
    d_qkv = jnp.concatenate([d_query, d_key, d_value], axis=1)
    d_proj = lax.dot_general(
        normed_low, d_qkv, (((0,), (0,)), ((), ())), preferred_element_type=F32
    ).astype(BF)
    d_normed = dot_t(d_qkv, proj_in)
    d_input_norm, d_gain_one = normalize_back(inputs, scale_one, gain_one, d_normed)
    grad_tokens = (d_resid + d_input_norm).astype(BF)

    d_small = jnp.concatenate(
        [
            d_gain_one[:, None],
            d_gain_two[:, None],
            d_router,
            jnp.pad(
                d_table.reshape(group_size, own_buckets, heads),
                ((0, 0), (0, shard - own_buckets), (0, 0)),
            ).reshape(width, heads),
            jnp.zeros((width, -used % 128), F32),
        ],
        axis=1,
    )
    order = ways[-1:] + others + ways[:-1]
    share_in, share_out, share_small = [
        sum_over(scatter_bits(value, order, keys, sizes), "rep", sizes["rep"])
        for value in (d_proj, d_proj_output, d_small)
    ]
    share_in = share_in.astype(F32)
    return (
        output,
        grad_tokens,
        share_small[:, 0],
        share_small[:, 1],
        share_in[:, :inner],
        share_in[:, inner : 2 * inner],
        share_in[:, 2 * inner :],
        share_out.astype(F32),
        share_small[:own_buckets, 2 + experts : used],
        share_small[:, 2 : 2 + experts],
        sum_in.astype(F32)[None],
        sum_out.astype(F32)[None],
    )


def solution(mesh):
    rows, group = P(("rep", "fsdp", "expert"), None), P(("fsdp", "expert"), None)
    flat_rows, flat_group = P(("rep", "fsdp", "expert")), P(("fsdp", "expert"))
    whole = P("expert", None, None)
    return jax.shard_map(
        functools.partial(body, dict(mesh.shape)),
        mesh=mesh,
        in_specs=(
            rows, rows, P(), rows, flat_rows, flat_group, flat_group,
            group, group, group, group, group, group, whole, whole, rows,
        ),
        out_specs=(
            rows, rows, flat_group, flat_group,
            group, group, group, group, group, group, whole, whole,
        ),
        check_vma=False,
    )
```

time: 614 us -> 428 us (0.70)
  waiting for transfers between devices: 325 us -> 106 us
  starting transfers between devices: 4.5 us -> 42.1 us
  other arithmetic: 26.1 us -> 44 us
  blocking collectives: 16 us -> 0 us
    psum x1, waiting for transfers between devices: 181 us -> 10.2 us  [body(): sum_in, sum_out = lax.psum((d_in, d_out), ('rep', 'fsdp'))]
    ppermute x0 -> x33, waiting for transfers between devices: none -> 80.6 us  [the longest x15 54.7 us: partner(): return lax.ppermute(value, axis, [(i, i ^ bit) for i in range(sizes[axis])])]
    reduce_scatter x2 -> x0, waiting for transfers between devices: 69.4 us -> none  [the longest x1 51.8 us: body(): share_in = lax.psum_scatter(d_proj, GROUP, scatter_dimension=0, tiled=True)]
    ppermute x0 -> x33, starting transfers between devices: none -> 36.8 us  [the longest x18 25.9 us: shift(): lax.ppermute(value, axis, [(i, (i + by) % size) for i in range(size)])]
    psum x1 -> x0, waiting for transfers between devices: 29.6 us -> none  [body(): lax.psum((share_out, share_in, share_small), 'rep')]
    all_gather x1 -> x0, waiting for transfers between devices: 28.6 us -> none  [body(): gathered = lax.all_gather(packed, GROUP, axis=0, tiled=True)]
    psum x1 -> x0, blocking collectives: 16 us -> none  [body(): lax.psum((share_out, share_in, share_small), 'rep')]
    pallas_call x3 -> x4, Pallas kernels: 63.4 us -> 71.9 us  [the longest x1 29.9 us: expert_gradients(): pl.pallas_call(functools.partial(gradients_kernel, experts), grid=(ff //...]
  transfers between devices with their start and end apart: 11 -> 39, of which waited for: 7 -> 17; matrix products, arithmetic and copies ran while one was open for 13% -> 24% of each run, Pallas kernels for 13% -> 21%
where the time goes in v1:
time: 428 us; the launch traced here: 420 us
  Pallas kernels  132 us (31%)
  waiting for transfers between devices  106 us (25%)
  matrix products  47.5 us (11%)
  other arithmetic  44 us (10%)
  starting transfers between devices  42.1 us (10%)
  local copies, waits for them, and re-layouts  32.9 us (8%)
  between operations  15.3 us (4%)
    ppermute x15, waiting for transfers between devices, partner(): return lax.ppermute(value, axis, [(i, i ^ bit) for i in range(sizes[axis])])  54.7 us
    pallas_call x1, Pallas kernels, attn_bwd(): pl.pallas_call(functools.partial(attn_bwd_kernel, head ** (-0.5), head),...  32 us
    dot_general x9, matrix products, dot32(): return jnp.dot(left, right, preferred_element_type=F32)  30.9 us
    pallas_call x1, Pallas kernels, expert_gradients(): pl.pallas_call(functools.partial(gradients_kernel, experts), grid=(ff //...  29.9 us
    pallas_call x2, Pallas kernels, expert_results(): pl.pallas_call(functools.partial(results_kernel, experts), grid=(ff // FF...  28.8 us
    pallas_call x1, Pallas kernels, attn_fwd(): pl.pallas_call(functools.partial(attn_fwd_kernel, head ** (-0.5), head),...  28.4 us
    ppermute x18, waiting for transfers between devices, shift(): lax.ppermute(value, axis, [(i, (i + by) % size) for i in range(size)])  25.9 us
    ppermute x18, starting transfers between devices, shift(): lax.ppermute(value, axis, [(i, (i + by) % size) for i in range(size)])  25.9 us
  transfers between devices with their start and end apart: 39, of which 17 were waited for; matrix products, arithmetic and copies ran while one was open for 24% of the time, Pallas kernels for 21%

profile of v1, /device:TPU:8, one launch (start us, length us, event | category | flops | bytes accessed | tf_op | source)
XLA Modules:
  0.0 420.3 jit_solution(18111231699689221395)
XLA Ops:
  12.4 1.5 collective-permute-start
  14.9 1.6 collective-permute-start.3
  16.4 1.6 select_convert_fusion.sq_ref
  18.0 1.6 fusion.50.sk_ref
  24.9 2.2 fusion.42
  27.2 2.3 fusion.36.g_ref
  30.8 1.7 copy.71
  37.5 1.4 maximum_select_fusion.7
  40.7 5.4 %collective-permute-done.4 = bf16[2,96,1152]{2,1,0:T(8,128)(2,1)S(1)} collective-permute-done((bf16[2,96,1152]{2,1,0:T(8,128)(2,1)S(1)}, bf16[2,96,1152]{2,1,0:T(8,128)(2,1)S(1)}, u32[]{:S(2)}, u32[]{:S(2)}) %collective-permute-start.4) | collective-permute-done | bytes 442400 | tf_op jit(solution)/shard_map/ppermute | solution.py:408
  46.4 4.8 %collective-permute-done.1 = bf16[2,96,1280]{2,1,0:T(8,128)(2,1)S(1)} collective-permute-done((bf16[2,96,1280]{2,1,0:T(8,128)(2,1)S(1)}, bf16[2,96,1280]{2,1,0:T(8,128)(2,1)S(1)}, u32[]{:S(2)}, u32[]{:S(2)}) %collective-permute-start.1) | collective-permute-done | bytes 491552 | tf_op jit(solution)/shard_map/ppermute | solution.py:408
  59.1 8.2 %convolution_convert_fusion.q_ref.k_ref.v_ref = bf16[1024,2304]{1,0:T(8,128)(2,1)} fusion(bf16[1024,768]{0,1:T(8,128)(2,1)S(1)} %copy.71, f32[768]{0:T(1024)S(1)} %get-tuple-element.103, f32[1024]{0:T(1024)S(1)} %get-tuple-element.130, bf16[768,1280]{1,0:T(8,128)(2,1)} %bitcast.185, bf16[768,1152]{1,0:T(8,128)(2,1)} %bitcast.194), kind=kOutput, calls=%fused_computation.6 | convolution fusion | flops 3636461568 | bytes 10034176 | tf_op jit(solution)/shard_map/dot_general | solution.py:399
  67.3 28.4 %attn_fwd.1 = (bf16[1024,768]{1,0:T(8,128)(2,1)}, f32[1024,768]{1,0:T(8,128)}, bf16[6,2,1024,1024]{3,2,1,0:T(8,128)(2,1)}) custom-call(bf16[1024,2304]{1,0:T(8,128)(2,1)} %convolution_convert_fusion.q_ref.k_ref.v_ref, bf16[1024,2304]{1,0:T(8,128)(2,1)} %convolution_convert_fusion.q_ref.k_ref.v_ref, ...), custom_call_target="tpu_custom_call" | custom-call | flops 16106127360 | bytes 25165824 | tf_op jit(solution)/shard_map/attn_fwd/pallas_call | solution.py:88
  95.7 3.5 multiply_reduce_fusion.2
  99.9 1.5 fusion.39
  101.4 2.4 fusion.33.x_ref.xl_ref
  103.8 1.5 collective-permute-start.6
  105.3 13.2 %expert_hidden.1 = (bf16[640,3072]{1,0:T(8,128)(2,1)}, bf16[640,3072]{1,0:T(8,128)(2,1)}, bf16[640,768]{1,0:T(8,128)(2,1)}) custom-call(bf16[640,768]{1,0:T(8,128)(2,1)} %fusion.33.x_ref.xl_ref, bf16[640,768]{1,0:T(8,128)(2,1)} %fusion.36.g_ref, bf16[768,128]{1,0:T(8,128)(2,1)} %pad.13.router_ref, f32[1,128]{1,0:T(1,128)} %compare_convert_fusion.mine_ref, ...), custom_call_target="tpu_custom_call" | custom-call | flops 12079595520 | bytes 17301504 | tf_op jit(solution)/shard_map/expert_hidden/pallas_call | solution.py:249
  118.5 9.2 %collective-permute-done.6.x_ref = bf16[640,768]{1,0:T(8,128)(2,1)S(1)} collective-permute-done((bf16[640,768]{1,0:T(8,128)(2,1)S(1)}, bf16[640,768]{1,0:T(8,128)(2,1)S(1)}, u32[]{:S(2)}, u32[]{:S(2)}) %collective-permute-start.6) | collective-permute-done | bytes 983072 | tf_op jit(solution)/shard_map/ppermute | solution.py:461
  128.6 29.9 %expert_gradients.1 = (bf16[640,3072]{1,0:T(8,128)(2,1)}, bf16[640,3072]{1,0:T(8,128)(2,1)}, bf16[640,768]{1,0:T(8,128)(2,1)}, bf16[768,3072]{1,0:T(8,128)(2,1)}, bf16[3072,768]{1,0:T(8,128)(2,1)}) custom-call(bf16[640,768]{1,0:T(8,128)(2,1)} %copy-done.31, bf16[640,768]{1,0:T(8,128)(2,1)} %collective-permute-done.7.g_ref, bf16[768,128]{1,0:T(8,128)(2,1)} %pad.13.router_ref, ...), custom_call_target="tpu_custom_call" | custom-call | flops 36238786560 | bytes 34603008 | tf_op jit(solution)/shard_map/expert_gradients/pallas_call | solution.py:291
  158.5 14.3 %expert_results.2 = (bf16[640,768]{1,0:T(8,128)(2,1)}, bf16[640,768]{1,0:T(8,128)(2,1)}, f32[128,768]{1,0:T(8,128)}) custom-call(bf16[640,768]{1,0:T(8,128)(2,1)} %copy-done.31, bf16[640,768]{1,0:T(8,128)(2,1)} %collective-permute-done.7.g_ref, bf16[768,128]{1,0:T(8,128)(2,1)} %pad.13.router_ref, f32[1,128]{1,0:T(1,128)} %compare_convert_fusion.mine_ref, ...), custom_call_target="tpu_custom_call" | custom-call | flops 12079595520 | bytes 17301504 | tf_op jit(solution)/shard_map/expert_results/pallas_call | solution.py:356
  172.8 1.5 collective-permute-start.8
  174.3 14.5 %expert_results.3 = (bf16[640,768]{1,0:T(8,128)(2,1)}, bf16[640,768]{1,0:T(8,128)(2,1)}, f32[128,768]{1,0:T(8,128)}) custom-call(bf16[640,768]{1,0:T(8,128)(2,1)} %fusion.33.x_ref.xl_ref, bf16[640,768]{1,0:T(8,128)(2,1)} %fusion.36.g_ref, bf16[768,128]{1,0:T(8,128)(2,1)} %pad.13.router_ref, f32[1,128]{1,0:T(1,128)} %compare_convert_fusion.mine_ref, ...), custom_call_target="tpu_custom_call" | custom-call | flops 12079595520 | bytes 17301504 | tf_op jit(solution)/shard_map/expert_results/pallas_call | solution.py:356
  189.9 6.2 %collective-permute-done.8 = bf16[640,768]{1,0:T(8,128)(2,1)} collective-permute-done((bf16[640,768]{1,0:T(8,128)(2,1)}, bf16[640,768]{1,0:T(8,128)(2,1)}, u32[]{:S(2)}, u32[]{:S(2)}) %collective-permute-start.8) | collective-permute-done | bytes 983072 | tf_op jit(solution)/shard_map/ppermute | solution.py:461
  196.2 6.7 %multiply_reduce_fusion = (f32[768]{0:T(1024)}, f32[1024]{0:T(1024)S(1)}, f32[1024,768]{0,1:T(8,128)S(1)}) fusion(f32[1024,768]{0,1:T(8,128)} %copy-done.5, f32[1024]{0:T(1024)S(1)} %copy-done.24, f32[768]{0:T(1024)S(1)} %get-tuple-element.102, bf16[640,768]{1,0:T(8,128)(2,1)} %collective-permute-done.8, bf16[640,768]{1,0:T(8,128)(2,1)} %get-tuple-element.52, ...), kind=kOutput, calls=%fused_computation.28 | convolution fusion | flops 2023225600 | bytes 8275968 | tf_op jit(solution)/shard_map/dot_general | solution.py:399
  204.1 2.6 convolution_convert_fusion.2.do_ref
  206.7 32.0 %attn_bwd.1 = (bf16[1024,768]{1,0:T(8,128)(2,1)}, bf16[1024,768]{1,0:T(8,128)(2,1)}, bf16[1024,768]{1,0:T(8,128)(2,1)}, f32[6,2,2048]{2,1,0:T(2,128)}) custom-call(bf16[1024,2304]{1,0:T(8,128)(2,1)} %convolution_convert_fusion.q_ref.k_ref.v_ref, bf16[1024,2304]{1,0:T(8,128)(2,1)} %convolution_convert_fusion.q_ref.k_ref.v_ref, ...), custom_call_target="tpu_custom_call" | custom-call | flops 16106127360 | bytes 25165824 | tf_op jit(solution)/shard_map/attn_bwd/pallas_call | solution.py:161
  238.8 1.7 constant_dynamic-update-slice_fusion.2
  243.0 5.8 %fusion.13 = (f32[768]{0:T(1024)S(1)}, f32[1024]{0:T(1024)S(1)}, f32[1024,768]{0,1:T(8,128)}) fusion(bf16[1024,768]{0,1:T(8,128)(2,1)S(1)} %copy.71, f32[1024]{0:T(1024)S(1)} %copy-done.21, f32[768]{0:T(1024)S(1)} %get-tuple-element.103, bf16[1024,2304]{1,0:T(8,128)(2,1)S(1)} %constant_dynamic-update-slice_fusion, bf16[768,1280]{1,0:T(8,128)(2,1)S(1)} %bitcast.186, ...), kind=kOutput, calls=%fused_computation.27 | convolution fusion | flops 3636459776 | bytes 13187072 | tf_op jit(solution)/shard_map/dot_general | solution.py:18
  248.7 5.5 %convolution_convert_fusion.1 = bf16[768,2304]{1,0:T(8,128)(2,1)} fusion(bf16[1024,2304]{1,0:T(8,128)(2,1)S(1)} %constant_dynamic-update-slice_fusion, bf16[1024,768]{0,1:T(8,128)(2,1)S(1)} %copy.71, f32[768]{0:T(1024)S(1)} %get-tuple-element.103, f32[1024]{0:T(1024)S(1)} %copy-done.21), kind=kOutput, calls=%fused_computation.11 | convolution fusion | flops 3628793856 | bytes 9837568 | tf_op jit(solution)/shard_map/dot_general | solution.py:612
  254.3 2.5 convolution_convert_fusion.3
  256.7 1.5 collective-permute-start.9
  260.1 1.6 concatenate.137
  261.8 1.4 collective-permute-done.10
  263.9 1.9 dynamic-slice_bitcast_fusion.2
  265.8 15.9 %collective-permute-done.11 = f32[2,96,128]{2,1,0:T(8,128)S(1)} collective-permute-done((f32[2,96,128]{2,1,0:T(8,128)S(1)}, f32[2,96,128]{2,1,0:T(8,128)S(1)}, u32[]{:S(2)}, u32[]{:S(2)}) %collective-permute-start.11) | collective-permute-done | bytes 98336 | tf_op jit(solution)/shard_map/ppermute | solution.py:408
  281.8 1.9 collective-permute-start.12
  283.6 3.8 fusion.10
  287.7 2.9 collective-permute-start.14
  290.6 2.5 collective-permute-start.13
  294.5 1.6 copy.91
  297.5 2.3 collective-permute-start.17
  301.3 1.5 collective-permute-start.29
  302.8 6.3 %collective-permute-done.29 = bf16[2,96,768]{2,1,0:T(8,128)(2,1)S(1)} collective-permute-done((bf16[2,96,768]{2,1,0:T(8,128)(2,1)S(1)}, bf16[2,96,768]{2,1,0:T(8,128)(2,1)S(1)}, u32[]{:S(2)}, u32[]{:S(2)}) %collective-permute-start.29) | collective-permute-done | bytes 294944 | tf_op jit(solution)/shard_map/ppermute | solution.py:408
  311.9 2.6 collective-permute-done.30
  314.6 2.3 fusion.3
  317.8 1.4 collective-permute-start.20
  319.9 2.2 collective-permute-start.33
  322.5 2.7 collective-permute-start.31
  325.2 3.9 add_convert_fusion
  329.1 1.6 copy.90
  334.5 2.0 collective-permute-done.20
  338.4 16.2 %collective-permute-done.21 = bf16[96,2304]{1,0:T(8,128)(2,1)S(1)} collective-permute-done((bf16[96,2304]{1,0:T(8,128)(2,1)S(1)}, bf16[96,2304]{1,0:T(8,128)(2,1)S(1)}, u32[]{:S(2)}, u32[]{:S(2)}) %collective-permute-start.21) | collective-permute-done | bytes 442400 | tf_op jit(solution)/shard_map/ppermute | solution.py:408
  355.9 2.2 collective-permute-start.23
  358.1 2.8 collective-permute-start.22
  361.0 3.2 collective-permute-done.24
  364.2 4.3 %collective-permute-done.23 = bf16[24,2304]{1,0:T(8,128)(2,1)S(1)} collective-permute-done((bf16[24,2304]{1,0:T(8,128)(2,1)S(1)}, bf16[24,2304]{1,0:T(8,128)(2,1)S(1)}, u32[]{:S(2)}, u32[]{:S(2)}) %collective-permute-start.23) | collective-permute-done | bytes 110624 | tf_op jit(solution)/shard_map/ppermute | solution.py:441
  368.5 5.7 %collective-permute-done.22 = bf16[24,2304]{1,0:T(8,128)(2,1)S(1)} collective-permute-done((bf16[24,2304]{1,0:T(8,128)(2,1)S(1)}, bf16[24,2304]{1,0:T(8,128)(2,1)S(1)}, u32[]{:S(2)}, u32[]{:S(2)}) %collective-permute-start.22) | collective-permute-done | bytes 110624 | tf_op jit(solution)/shard_map/ppermute | solution.py:441
  375.1 1.9 collective-permute-start.26
  377.1 5.5 %collective-permute-done.25 = bf16[24,2304]{1,0:T(8,128)(2,1)S(1)} collective-permute-done((bf16[24,2304]{1,0:T(8,128)(2,1)S(1)}, bf16[24,2304]{1,0:T(8,128)(2,1)S(1)}, u32[]{:S(2)}, u32[]{:S(2)}) %collective-permute-start.25) | collective-permute-done | bytes 110624 | tf_op jit(solution)/shard_map/ppermute | solution.py:441
  382.6 3.7 collective-permute-done.26
  386.4 3.4 collective-permute-done.27
  390.8 10.2 %all-reduce.6.cloned.1.call-done = (bf16[1,768,3072]{2,1,0:T(8,128)(2,1)}, bf16[1,3072,768]{2,1,0:T(8,128)(2,1)}) async-done(((bf16[1,768,3072]{2,1,0:T(8,128)(2,1)}, bf16[1,3072,768]{2,1,0:T(8,128)(2,1)}), (bf16[1,768,3072]{2,1,0:T(8,128)(2,1)}, bf16[1,3072,768]{2,1,0:T(8,128)(2,1)})) %all-reduce.6.cloned.1.call-update) | async-done | bytes 9437200 | tf_op jit(solution)/shard_map/psum | solution.py:579
  401.0 7.5 %broadcast_in_dim.126 = f32[1,768,3072]{2,1,0:T(8,128)} convert(bf16[1,768,3072]{2,1,0:T(8,128)(2,1)} %get-tuple-element.106) | non-fusion elementwise | flops 2359296 | bytes 14155776 | tf_op jit(solution)/shard_map/broadcast_in_dim | solution.py:649
  408.5 4.5 %broadcast_in_dim.128 = f32[1,3072,768]{2,1,0:T(8,128)} convert(bf16[1,3072,768]{2,1,0:T(8,128)(2,1)S(1)} %copy-done.1) | non-fusion elementwise | flops 2359296 | bytes 14155776 | tf_op jit(solution)/shard_map/broadcast_in_dim | solution.py:650
  (218 shorter events, 54.9 us)
Async XLA Ops:
  7.2 17.8 %copy-start.10 = (bf16[1024,768]{1,0:T(8,128)(2,1)S(1)}, bf16[1024,768]{1,0:T(8,128)(2,1)}, u32[]{:S(2)}) copy-start(bf16[1024,768]{1,0:T(8,128)(2,1)} %param.31) | copy-start | bytes 4718596
  7.2 88.5 %all-gather.2.cloned.1.call-start = ((), (), s32[]{:S(2)}) async-start(), calls=%async_computation | async-start | bytes 1327104 | tf_op jit(solution)/shard_map/all_gather | solution.py:531
  12.4 25.2 %collective-permute-start = (bf16[96,1280]{1,0:T(8,128)(2,1)}, bf16[96,1280]{1,0:T(8,128)(2,1)}, u32[]{:S(2)}, u32[]{:S(2)}) collective-permute-start(bf16[96,1280]{1,0:T(8,128)(2,1)} %get-tuple-element.122), channel_id=1, source_target_pairs={{0,4},{2,6},{4,0},{6,2},{1,5},{3,7},{5,1},{7,3},{8,12},{10,14},{12... | collective-permute-start | bytes 737288 | tf_op jit(solution)/shard_map/ppermute | solution.py:408
  14.9 18.7 %collective-permute-start.3 = (bf16[96,1152]{1,0:T(8,128)(2,1)S(1)}, bf16[96,1152]{1,0:T(8,128)(2,1)}, u32[]{:S(2)}, u32[]{:S(2)}) collective-permute-start(bf16[96,1152]{1,0:T(8,128)(2,1)S(1)} %pad_maximum_fusion.1), channel_id=1, source_target_pairs={{0,1},{1,0},{2,3},{3,2},{4,5},{5,4},{6,7},{7,6},{8,9},{9,8},{10,11... | collective-permute-start | bytes 663560 | tf_op jit(solution)/shard_map/ppermute | solution.py:408
  30.2 2.7 copy-start.28
  33.0 23.6 %copy-start.17 = (s32[2048]{0:T(1024)}, s32[2048]{0:T(1024)S(1)}, u32[]{:S(2)}) copy-start(s32[2048]{0:T(1024)S(1)} %pad_add_fusion) | copy-start | bytes 24580
  33.0 6.6 %copy-start.8 = (bf16[1,1,96,1280]{3,2,0,1:T(8,128)(2,1)S(1)}, bf16[1,1,96,1280]{3,2,0,1:T(8,128)(2,1)}, u32[]{:S(2)}) copy-start(bf16[1,1,96,1280]{3,2,0,1:T(8,128)(2,1)} %get-tuple-element.120) | copy-start | bytes 737284
  33.6 25.5 %copy-start.20 = (f32[1024]{0:T(1024)}, f32[1024]{0:T(1024)S(1)}, u32[]{:S(2)}) copy-start(f32[1024]{0:T(1024)S(1)} %get-tuple-element.130) | copy-start | bytes 12292
  34.7 11.4 %collective-permute-start.4 = (bf16[2,96,1152]{2,1,0:T(8,128)(2,1)S(1)}, bf16[2,96,1152]{2,1,0:T(8,128)(2,1)S(1)}, u32[]{:S(2)}, u32[]{:S(2)}) collective-permute-start(bf16[2,96,1152]{2,1,0:T(8,128)(2,1)S(1)} %maximum_select_fusion.9), channel_id=1, source_target_pairs={{0,4},{2,6},{4,0},{6,2},{1,5},{3,7},{5,1},{7,3},{8,12},{10,14},{12... | collective-permute-start | bytes 1327112 | tf_op jit(solution)/shard_map/ppermute | solution.py:408
  38.9 12.2 %collective-permute-start.1 = (bf16[2,96,1280]{2,1,0:T(8,128)(2,1)S(1)}, bf16[2,96,1280]{2,1,0:T(8,128)(2,1)S(1)}, u32[]{:S(2)}, u32[]{:S(2)}) collective-permute-start(bf16[2,96,1280]{2,1,0:T(8,128)(2,1)S(1)} %maximum_select_fusion.7), channel_id=1, source_target_pairs={{0,1},{1,0},{2,3},{3,2},{4,5},{5,4},{6,7},{7,6},{8,9},{9,8},{10,11... | collective-permute-start | bytes 1474568 | tf_op jit(solution)/shard_map/ppermute | solution.py:408
  46.3 6.6 %collective-permute-start.5 = (bf16[2,2,96,1152]{3,2,1,0:T(8,128)(2,1)S(1)}, bf16[2,2,96,1152]{3,2,1,0:T(8,128)(2,1)S(1)}, u32[]{:S(2)}, u32[]{:S(2)}) collective-permute-start(bf16[2,2,96,1152]{3,2,1,0:T(8,128)(2,1)S(1)} %maximum_select_fusion.5), channel_id=1, source_target_pairs={{0,2},{2,0},{4,6},{6,4},{1,3},{3,1},{5,7},{7,5},{8,10},{10,8},{12,... | collective-permute-start | bytes 2654216 | tf_op jit(solution)/shard_map/ppermute | solution.py:408
  51.3 3.2 collective-permute-start.2
  57.5 343.5 %all-reduce.6.cloned.1.call-start = ((), (), s32[]{:S(2)}) async-start(), calls=%async_computation.1 | async-start | bytes 18874368 | tf_op jit(solution)/shard_map/psum | solution.py:579
  57.8 60.7 %collective-permute-start.7 = (bf16[640,768]{1,0:T(8,128)(2,1)}, bf16[640,768]{1,0:T(8,128)(2,1)}, u32[]{:S(2)}, u32[]{:S(2)}) collective-permute-start(bf16[640,768]{1,0:T(8,128)(2,1)} %fusion.42), channel_id=1, source_target_pairs={{0,1},{1,0},{2,3},{3,2},{4,5},{5,4},{6,7},{7,6},{8,9},{9,8},{10,11... | collective-permute-start | bytes 2949128 | tf_op jit(solution)/shard_map/ppermute | solution.py:461
  95.7 4.2 copy-start.14
  103.8 23.9 %collective-permute-start.6 = (bf16[640,768]{1,0:T(8,128)(2,1)S(1)}, bf16[640,768]{1,0:T(8,128)(2,1)S(1)}, u32[]{:S(2)}, u32[]{:S(2)}) collective-permute-start(bf16[640,768]{1,0:T(8,128)(2,1)S(1)} %fusion.39), channel_id=1, source_target_pairs={{0,1},{1,0},{2,3},{3,2},{4,5},{5,4},{6,7},{7,6},{8,9},{9,8},{10,11... | collective-permute-start | bytes 2949128 | tf_op jit(solution)/shard_map/ppermute | solution.py:461
  172.8 23.3 %collective-permute-start.8 = (bf16[640,768]{1,0:T(8,128)(2,1)}, bf16[640,768]{1,0:T(8,128)(2,1)}, u32[]{:S(2)}, u32[]{:S(2)}) collective-permute-start(bf16[640,768]{1,0:T(8,128)(2,1)} %get-tuple-element.47), channel_id=1, source_target_pairs={{0,1},{1,0},{2,3},{3,2},{4,5},{5,4},{6,7},{7,6},{8,9},{9,8},{10,11... | collective-permute-start | bytes 2949128 | tf_op jit(solution)/shard_map/ppermute | solution.py:461
  189.9 6.3 %copy-start.24 = (f32[1024]{0:T(1024)S(1)}, f32[1024]{0:T(1024)}, u32[]{:S(2)}) copy-start(f32[1024]{0:T(1024)} %copy-done.23) | copy-start | bytes 12292
  196.2 6.7 %copy-start.6 = (f32[1024,768]{0,1:T(8,128)S(1)}, f32[1024,768]{0,1:T(8,128)}, u32[]{:S(2)}) copy-start(f32[1024,768]{0,1:T(8,128)} %copy-done.5) | copy-start | bytes 9437188
  196.2 6.7 %copy-start.22 = (f32[1024]{0:T(1024)S(1)}, f32[1024]{0:T(1024)}, u32[]{:S(2)}) copy-start(f32[1024]{0:T(1024)} %get-tuple-element.131) | copy-start | bytes 12292
  204.1 50.1 %copy-start = (f32[1024,768]{0,1:T(8,128)}, f32[1024,768]{0,1:T(8,128)S(1)}, u32[]{:S(2)}) copy-start(f32[1024,768]{0,1:T(8,128)S(1)} %subtract_add_fusion) | copy-start | bytes 9437188
  238.8 2.4 copy-start.11
  240.7 2.3 copy-start.9
  240.7 2.3 copy-start.21
  248.7 5.5 %copy-start.32 = (bf16[1024,768]{1,0:T(8,128)(2,1)S(1)}, bf16[1024,768]{1,0:T(8,128)(2,1)}, u32[]{:S(2)}) copy-start(bf16[1024,768]{1,0:T(8,128)(2,1)} %get-tuple-element.37.o_ref) | copy-start | bytes 4718596
  254.2 4.2 %copy-start.29 = (f32[768]{0:T(1024)S(1)}, f32[768]{0:T(1024)}, u32[]{:S(2)}) copy-start(f32[768]{0:T(1024)} %get-tuple-element.98) | copy-start | bytes 9220
  254.2 4.5 %copy-start.16 = (f32[6,2,2048]{2,1,0:T(2,128)S(1)}, f32[6,2,2048]{2,1,0:T(2,128)}, u32[]{:S(2)}) copy-start(f32[6,2,2048]{2,1,0:T(2,128)} %get-tuple-element.60) | copy-start | bytes 294916
  254.2 4.6 %copy-start.18 = (s32[2048]{0:T(1024)S(1)}, s32[2048]{0:T(1024)}, u32[]{:S(2)}) copy-start(s32[2048]{0:T(1024)} %copy-done.17) | copy-start | bytes 24580
  254.3 4.6 %copy-start.27 = (s32[8,4]{0,1:T(4,128)S(1)}, s32[8,4]{0,1:T(4,128)}, u32[]{:S(2)}) copy-start(s32[8,4]{0,1:T(4,128)} %multiply_add_fusion) | copy-start | bytes 388
  256.7 68.4 %collective-permute-start.9 = (bf16[640,768]{1,0:T(8,128)(2,1)}, bf16[640,768]{1,0:T(8,128)(2,1)}, u32[]{:S(2)}, u32[]{:S(2)}) collective-permute-start(bf16[640,768]{1,0:T(8,128)(2,1)} %get-tuple-element.51), channel_id=1, source_target_pairs={{0,1},{1,0},{2,3},{3,2},{4,5},{5,4},{6,7},{7,6},{8,9},{9,8},{10,11... | collective-permute-start | bytes 2949128 | tf_op jit(solution)/shard_map/ppermute | solution.py:461
  259.2 24.4 %copy-start.19 = (f32[1024]{0:T(1024)S(1)}, f32[1024]{0:T(1024)}, u32[]{:S(2)}) copy-start(f32[1024]{0:T(1024)} %get-tuple-element.129) | copy-start | bytes 12292
  261.7 1.5 collective-permute-start.10
  263.3 18.5 %collective-permute-start.11 = (f32[2,96,128]{2,1,0:T(8,128)S(1)}, f32[2,96,128]{2,1,0:T(8,128)S(1)}, u32[]{:S(2)}, u32[]{:S(2)}) collective-permute-start(f32[2,96,128]{2,1,0:T(8,128)S(1)} %dynamic-slice_bitcast_fusion.10), channel_id=1, source_target_pairs={{0,1},{1,0},{2,3},{3,2},{4,5},{5,4},{6,7},{7,6},{8,9},{9,8},{10,11... | collective-permute-start | bytes 294920 | tf_op jit(solution)/shard_map/ppermute | solution.py:408
  265.8 34.0 %collective-permute-start.28 = (bf16[2,2,96,768]{3,2,1,0:T(8,128)(2,1)}, bf16[2,2,96,768]{3,2,1,0:T(8,128)(2,1)}, u32[]{:S(2)}, u32[]{:S(2)}) collective-permute-start(bf16[2,2,96,768]{3,2,1,0:T(8,128)(2,1)} %dynamic-slice_bitcast_fusion.2), channel_id=1, source_target_pairs={{0,2},{2,0},{4,6},{6,4},{1,3},{3,1},{5,7},{7,5},{8,10},{10,8},{12,... | collective-permute-start | bytes 1769480 | tf_op jit(solution)/shard_map/ppermute | solution.py:408
  281.8 5.6 %collective-permute-start.12 = (f32[96,128]{1,0:T(8,128)S(1)}, f32[96,128]{1,0:T(8,128)S(1)}, u32[]{:S(2)}, u32[]{:S(2)}) collective-permute-start(f32[96,128]{1,0:T(8,128)S(1)} %dynamic-slice_bitcast_fusion.11), channel_id=1, source_target_pairs={{0,4},{2,6},{4,0},{6,2},{1,5},{3,7},{5,1},{7,3},{8,12},{10,14},{12... | collective-permute-start | bytes 147464 | tf_op jit(solution)/shard_map/ppermute | solution.py:408
  283.6 9.5 %copy-start.4 = (bf16[768,2304]{1,0:T(8,128)(2,1)S(1)}, bf16[768,2304]{1,0:T(8,128)(2,1)}, u32[]{:S(2)}) copy-start(bf16[768,2304]{1,0:T(8,128)(2,1)} %convolution_convert_fusion.1) | copy-start | bytes 10616836
  287.5 8.6 %collective-permute-start.15 = (f32[24,128]{1,0:T(8,128)S(1)}, f32[24,128]{1,0:T(8,128)S(1)}, u32[]{:S(2)}, u32[]{:S(2)}) collective-permute-start(f32[24,128]{1,0:T(8,128)S(1)} %get-tuple-element.127), channel_id=1, source_target_pairs={{0,24},{8,0},{16,8},{24,16},{1,25},{9,1},{17,9},{25,17},{2,26},{10... | collective-permute-start | bytes 36872 | tf_op jit(solution)/shard_map/ppermute | solution.py:441
  287.7 8.3 %collective-permute-start.14 = (f32[24,128]{1,0:T(8,128)S(1)}, f32[24,128]{1,0:T(8,128)S(1)}, u32[]{:S(2)}, u32[]{:S(2)}) collective-permute-start(f32[24,128]{1,0:T(8,128)S(1)} %get-tuple-element.128), channel_id=1, source_target_pairs={{0,16},{8,24},{16,0},{24,8},{1,17},{9,25},{17,1},{25,9},{2,18},{10... | collective-permute-start | bytes 36872 | tf_op jit(solution)/shard_map/ppermute | solution.py:441
  290.6 5.4 %collective-permute-start.13 = (f32[24,128]{1,0:T(8,128)S(1)}, f32[24,128]{1,0:T(8,128)S(1)}, u32[]{:S(2)}, u32[]{:S(2)}) collective-permute-start(f32[24,128]{1,0:T(8,128)S(1)} %get-tuple-element.126), channel_id=1, source_target_pairs={{0,8},{8,16},{16,24},{24,0},{1,9},{9,17},{17,25},{25,1},{2,10},{10... | collective-permute-start | bytes 36872 | tf_op jit(solution)/shard_map/ppermute | solution.py:441
  296.0 18.5 %collective-permute-start.19 = (bf16[2,2,96,2304]{3,2,1,0:T(8,128)(2,1)}, bf16[2,2,96,2304]{3,2,1,0:T(8,128)(2,1)S(1)}, u32[]{:S(2)}, u32[]{:S(2)}) collective-permute-start(bf16[2,2,96,2304]{3,2,1,0:T(8,128)(2,1)} %dynamic-slice_bitcast_fusion), channel_id=1, source_target_pairs={{0,2},{2,0},{4,6},{6,4},{1,3},{3,1},{5,7},{7,5},{8,10},{10,8},{12,... | collective-permute-start | bytes 5308424 | tf_op jit(solution)/shard_map/ppermute | solution.py:408
  296.1 5.2 %collective-permute-start.16 = (f32[24,128]{1,0:T(8,128)S(1)}, f32[24,128]{1,0:T(8,128)S(1)}, u32[]{:S(2)}, u32[]{:S(2)}) collective-permute-start(f32[24,128]{1,0:T(8,128)S(1)} %get-tuple-element.113), channel_id=1, source_target_pairs={{0,8},{8,16},{16,24},{24,0},{1,9},{9,17},{17,25},{25,1},{2,10},{10... | collective-permute-start | bytes 36872 | tf_op jit(solution)/shard_map/ppermute | solution.py:441
  297.5 5.3 %collective-permute-start.17 = (f32[24,128]{1,0:T(8,128)S(1)}, f32[24,128]{1,0:T(8,128)S(1)}, u32[]{:S(2)}, u32[]{:S(2)}) collective-permute-start(f32[24,128]{1,0:T(8,128)S(1)} %get-tuple-element.113), channel_id=1, source_target_pairs={{0,16},{8,24},{16,0},{24,8},{1,17},{9,25},{17,1},{25,9},{2,18},{10... | collective-permute-start | bytes 36872 | tf_op jit(solution)/shard_map/ppermute | solution.py:441
  299.9 10.0 %collective-permute-start.18 = (f32[24,128]{1,0:T(8,128)S(1)}, f32[24,128]{1,0:T(8,128)S(1)}, u32[]{:S(2)}, u32[]{:S(2)}) collective-permute-start(f32[24,128]{1,0:T(8,128)S(1)} %get-tuple-element.113), channel_id=1, source_target_pairs={{0,24},{8,0},{16,8},{24,16},{1,25},{9,1},{17,9},{25,17},{2,26},{10... | collective-permute-start | bytes 36872 | tf_op jit(solution)/shard_map/ppermute | solution.py:441
  301.3 7.9 %collective-permute-start.29 = (bf16[2,96,768]{2,1,0:T(8,128)(2,1)S(1)}, bf16[2,96,768]{2,1,0:T(8,128)(2,1)S(1)}, u32[]{:S(2)}, u32[]{:S(2)}) collective-permute-start(bf16[2,96,768]{2,1,0:T(8,128)(2,1)S(1)} %dynamic-slice_bitcast_fusion.4), channel_id=1, source_target_pairs={{0,1},{1,0},{2,3},{3,2},{4,5},{5,4},{6,7},{7,6},{8,9},{9,8},{10,11... | collective-permute-start | bytes 884744 | tf_op jit(solution)/shard_map/ppermute | solution.py:408
  309.3 5.2 %collective-permute-start.30 = (bf16[96,768]{1,0:T(8,128)(2,1)S(1)}, bf16[96,768]{1,0:T(8,128)(2,1)S(1)}, u32[]{:S(2)}, u32[]{:S(2)}) collective-permute-start(bf16[96,768]{1,0:T(8,128)(2,1)S(1)} %dynamic-slice_bitcast_fusion.6), channel_id=1, source_target_pairs={{0,4},{2,6},{4,0},{6,2},{1,5},{3,7},{5,1},{7,3},{8,12},{10,14},{12... | collective-permute-start | bytes 442376 | tf_op jit(solution)/shard_map/ppermute | solution.py:408
  314.5 4.8 %copy-start.15 = (bf16[96,768]{1,0:T(8,128)(2,1)}, bf16[96,768]{1,0:T(8,128)(2,1)S(1)}, u32[]{:S(2)}) copy-start(bf16[96,768]{1,0:T(8,128)(2,1)S(1)} %fusion.53) | copy-start | bytes 442372
  314.5 10.6 %copy-start.7 = (f32[1024,768]{0,1:T(8,128)S(1)}, f32[1024,768]{0,1:T(8,128)}, u32[]{:S(2)}) copy-start(f32[1024,768]{0,1:T(8,128)} %copy-done.5) | copy-start | bytes 9437188
  314.5 10.6 %copy-start.26 = (s32[1024]{0:T(1024)S(1)}, s32[1024]{0:T(1024)}, u32[]{:S(2)}) copy-start(s32[1024]{0:T(1024)} %copy-done.25) | copy-start | bytes 12292
  314.5 10.6 %copy-start.33 = (bf16[640,768]{1,0:T(8,128)(2,1)S(1)}, bf16[640,768]{1,0:T(8,128)(2,1)}, u32[]{:S(2)}) copy-start(bf16[640,768]{1,0:T(8,128)(2,1)} %get-tuple-element.49) | copy-start | bytes 2949124
  317.8 18.6 %collective-permute-start.20 = (bf16[2,96,2304]{2,1,0:T(8,128)(2,1)}, bf16[2,96,2304]{2,1,0:T(8,128)(2,1)}, u32[]{:S(2)}, u32[]{:S(2)}) collective-permute-start(bf16[2,96,2304]{2,1,0:T(8,128)(2,1)} %dynamic-slice_bitcast_fusion.1), channel_id=1, source_target_pairs={{0,1},{1,0},{2,3},{3,2},{4,5},{5,4},{6,7},{7,6},{8,9},{9,8},{10,11... | collective-permute-start | bytes 2654216 | tf_op jit(solution)/shard_map/ppermute | solution.py:408
  319.9 10.8 %collective-permute-start.33 = (bf16[24,768]{1,0:T(8,128)(2,1)}, bf16[24,768]{1,0:T(8,128)(2,1)S(1)}, u32[]{:S(2)}, u32[]{:S(2)}) collective-permute-start(bf16[24,768]{1,0:T(8,128)(2,1)} %get-tuple-element.124), channel_id=1, source_target_pairs={{0,24},{8,0},{16,8},{24,16},{1,25},{9,1},{17,9},{25,17},{2,26},{10... | collective-permute-start | bytes 110600 | tf_op jit(solution)/shard_map/ppermute | solution.py:441
  322.1 8.6 %collective-permute-start.32 = (bf16[24,768]{1,0:T(8,128)(2,1)S(1)}, bf16[24,768]{1,0:T(8,128)(2,1)S(1)}, u32[]{:S(2)}, u32[]{:S(2)}) collective-permute-start(bf16[24,768]{1,0:T(8,128)(2,1)S(1)} %get-tuple-element.125), channel_id=1, source_target_pairs={{0,16},{8,24},{16,0},{24,8},{1,17},{9,25},{17,1},{25,9},{2,18},{10... | collective-permute-start | bytes 110600 | tf_op jit(solution)/shard_map/ppermute | solution.py:441
  322.5 8.2 %collective-permute-start.31 = (bf16[24,768]{1,0:T(8,128)(2,1)S(1)}, bf16[24,768]{1,0:T(8,128)(2,1)S(1)}, u32[]{:S(2)}, u32[]{:S(2)}) collective-permute-start(bf16[24,768]{1,0:T(8,128)(2,1)S(1)} %get-tuple-element.123), channel_id=1, source_target_pairs={{0,8},{8,16},{16,24},{24,0},{1,9},{9,17},{17,25},{25,1},{2,10},{10... | collective-permute-start | bytes 110600 | tf_op jit(solution)/shard_map/ppermute | solution.py:441
  331.5 6.9 %collective-permute-start.34 = (bf16[24,768]{1,0:T(8,128)(2,1)S(1)}, bf16[24,768]{1,0:T(8,128)(2,1)S(1)}, u32[]{:S(2)}, u32[]{:S(2)}) collective-permute-start(bf16[24,768]{1,0:T(8,128)(2,1)S(1)} %get-tuple-element.109), channel_id=1, source_target_pairs={{0,8},{8,16},{16,24},{24,0},{1,9},{9,17},{17,25},{25,1},{2,10},{10... | collective-permute-start | bytes 110600 | tf_op jit(solution)/shard_map/ppermute | solution.py:441
  332.2 6.1 %collective-permute-start.35 = (bf16[24,768]{1,0:T(8,128)(2,1)S(1)}, bf16[24,768]{1,0:T(8,128)(2,1)S(1)}, u32[]{:S(2)}, u32[]{:S(2)}) collective-permute-start(bf16[24,768]{1,0:T(8,128)(2,1)S(1)} %get-tuple-element.109), channel_id=1, source_target_pairs={{0,16},{8,24},{16,0},{24,8},{1,17},{9,25},{17,1},{25,9},{2,18},{10... | collective-permute-start | bytes 110600 | tf_op jit(solution)/shard_map/ppermute | solution.py:441
  333.6 27.3 %collective-permute-start.36 = (bf16[24,768]{1,0:T(8,128)(2,1)S(1)}, bf16[24,768]{1,0:T(8,128)(2,1)S(1)}, u32[]{:S(2)}, u32[]{:S(2)}) collective-permute-start(bf16[24,768]{1,0:T(8,128)(2,1)S(1)} %get-tuple-element.109), channel_id=1, source_target_pairs={{0,24},{8,0},{16,8},{24,16},{1,25},{9,1},{17,9},{25,17},{2,26},{10... | collective-permute-start | bytes 110600 | tf_op jit(solution)/shard_map/ppermute | solution.py:441
  337.9 16.7 %collective-permute-start.21 = (bf16[96,2304]{1,0:T(8,128)(2,1)S(1)}, bf16[96,2304]{1,0:T(8,128)(2,1)S(1)}, u32[]{:S(2)}, u32[]{:S(2)}) collective-permute-start(bf16[96,2304]{1,0:T(8,128)(2,1)S(1)} %dynamic-slice_bitcast_fusion.3), channel_id=1, source_target_pairs={{0,4},{2,6},{4,0},{6,2},{1,5},{3,7},{5,1},{7,3},{8,12},{10,14},{12... | collective-permute-start | bytes 1327112 | tf_op jit(solution)/shard_map/ppermute | solution.py:408
  354.8 9.4 %collective-permute-start.24 = (bf16[24,2304]{1,0:T(8,128)(2,1)S(1)}, bf16[24,2304]{1,0:T(8,128)(2,1)S(1)}, u32[]{:S(2)}, u32[]{:S(2)}) collective-permute-start(bf16[24,2304]{1,0:T(8,128)(2,1)S(1)} %get-tuple-element.118), channel_id=1, source_target_pairs={{0,24},{8,0},{16,8},{24,16},{1,25},{9,1},{17,9},{25,17},{2,26},{10... | collective-permute-start | bytes 331784 | tf_op jit(solution)/shard_map/ppermute | solution.py:441
  355.9 12.6 %collective-permute-start.23 = (bf16[24,2304]{1,0:T(8,128)(2,1)S(1)}, bf16[24,2304]{1,0:T(8,128)(2,1)S(1)}, u32[]{:S(2)}, u32[]{:S(2)}) collective-permute-start(bf16[24,2304]{1,0:T(8,128)(2,1)S(1)} %get-tuple-element.119), channel_id=1, source_target_pairs={{0,16},{8,24},{16,0},{24,8},{1,17},{9,25},{17,1},{25,9},{2,18},{10... | collective-permute-start | bytes 331784 | tf_op jit(solution)/shard_map/ppermute | solution.py:441
  358.1 16.1 %collective-permute-start.22 = (bf16[24,2304]{1,0:T(8,128)(2,1)S(1)}, bf16[24,2304]{1,0:T(8,128)(2,1)S(1)}, u32[]{:S(2)}, u32[]{:S(2)}) collective-permute-start(bf16[24,2304]{1,0:T(8,128)(2,1)S(1)} %get-tuple-element.117), channel_id=1, source_target_pairs={{0,8},{8,16},{16,24},{24,0},{1,9},{9,17},{17,25},{25,1},{2,10},{10... | collective-permute-start | bytes 331784 | tf_op jit(solution)/shard_map/ppermute | solution.py:441
  374.3 8.3 %collective-permute-start.25 = (bf16[24,2304]{1,0:T(8,128)(2,1)S(1)}, bf16[24,2304]{1,0:T(8,128)(2,1)S(1)}, u32[]{:S(2)}, u32[]{:S(2)}) collective-permute-start(bf16[24,2304]{1,0:T(8,128)(2,1)S(1)} %get-tuple-element.111), channel_id=1, source_target_pairs={{0,8},{8,16},{16,24},{24,0},{1,9},{9,17},{17,25},{25,1},{2,10},{10... | collective-permute-start | bytes 331784 | tf_op jit(solution)/shard_map/ppermute | solution.py:441
  375.1 11.3 %collective-permute-start.26 = (bf16[24,2304]{1,0:T(8,128)(2,1)S(1)}, bf16[24,2304]{1,0:T(8,128)(2,1)S(1)}, u32[]{:S(2)}, u32[]{:S(2)}) collective-permute-start(bf16[24,2304]{1,0:T(8,128)(2,1)S(1)} %get-tuple-element.111), channel_id=1, source_target_pairs={{0,16},{8,24},{16,0},{24,8},{1,17},{9,25},{17,1},{25,9},{2,18},{10... | collective-permute-start | bytes 331784 | tf_op jit(solution)/shard_map/ppermute | solution.py:441
  377.0 12.8 %collective-permute-start.27 = (bf16[24,2304]{1,0:T(8,128)(2,1)S(1)}, bf16[24,2304]{1,0:T(8,128)(2,1)S(1)}, u32[]{:S(2)}, u32[]{:S(2)}) collective-permute-start(bf16[24,2304]{1,0:T(8,128)(2,1)S(1)} %get-tuple-element.111), channel_id=1, source_target_pairs={{0,24},{8,0},{16,8},{24,16},{1,25},{9,1},{17,9},{25,17},{2,26},{10... | collective-permute-start | bytes 331784 | tf_op jit(solution)/shard_map/ppermute | solution.py:441
  401.0 7.5 %copy-start.1 = (bf16[1,3072,768]{2,1,0:T(8,128)(2,1)S(1)}, bf16[1,3072,768]{2,1,0:T(8,128)(2,1)}, u32[]{:S(2)}) copy-start(bf16[1,3072,768]{2,1,0:T(8,128)(2,1)} %get-tuple-element.107) | copy-start | bytes 14155780
  (9 other events, 13.7 us)
Sparse Core Ops, SparseCore 0:
  57.6 29.2 all-gather.1
  190.0 210.9 all-reduce.5

commit v2 on v1

--- a/solution.py
+++ b/solution.py
@@ -172,8 +172,8 @@
         + [pltpu.VMEM((2 * head, length), F32)] * 2,
         compiler_params=pltpu.CompilerParams(vmem_limit_bytes=VMEM_BYTES),
         cost_estimate=pl.CostEstimate(
-            flops=40 * heads * length * length * head // 2,
-            bytes_accessed=2 * heads * length * length,
+            flops=4 * heads * length * length * head // 2,
+            bytes_accessed=heads * length * length // 4,
             transcendentals=0,
         ),
         name="attn_bwd",
@@ -217,164 +217,135 @@
     deo_ref[...] = (gate * g_ref[...].astype(F32)).astype(BF)
 
 
-def hidden_kernel(
-    experts, x_ref, g_ref, router_ref, mine_ref, win_ref, wout_ref, act_ref, du_ref, deo_ref
+def fixed(*shape):
+    return pl.BlockSpec(shape, lambda f: (0,) * len(shape))
+
+
+def in_block(width):
+    return pl.BlockSpec((1, width, FF_BLOCK), lambda f: (0, 0, f))
+
+
+def out_block(width):
+    return pl.BlockSpec((1, FF_BLOCK, width), lambda f: (0, f, 0))
+
+
+def slot_block(rows):
+    return pl.BlockSpec((rows, FF_BLOCK), lambda f: (0, f))
+
+
+def expert_kernel(
+    experts, x_ref, g_ref, router_ref, mine_ref, win_ref, wout_ref,
+    act_ref, du_ref, deo_ref, geo_ref, dn_ref, drouter_ref, eo, dx,
 ):
     @pl.when(pl.program_id(0) == 0)
     def _():
         gated_cotangent(experts, x_ref, g_ref, router_ref, mine_ref, deo_ref)
+        eo[...] = jnp.zeros_like(eo)
+        dx[...] = jnp.zeros_like(dx)
 
     hidden_step(x_ref, deo_ref, win_ref, wout_ref, act_ref, du_ref)
-
-
-def fixed(*shape):
-    return pl.BlockSpec(shape, lambda f: (0,) * len(shape))
-
-
-def in_block(width):
-    return pl.BlockSpec((1, width, FF_BLOCK), lambda f: (0, 0, f))
-
-
-def out_block(width):
-    return pl.BlockSpec((1, FF_BLOCK, width), lambda f: (0, f, 0))
-
-
-def slot_block(rows):
-    return pl.BlockSpec((rows, FF_BLOCK), lambda f: (0, f))
-
-
-def expert_hidden(x, g, router, mine, win, wout, experts):
+    eo[...] += dot_n(act_ref[...], wout_ref[0])
+    dx[...] += dot_t(du_ref[...], win_ref[0])
+
+    @pl.when(pl.program_id(0) == pl.num_programs(0) - 1)
+    def _():
+        finish(experts, x_ref, g_ref, router_ref, mine_ref, eo, dx, geo_ref, dn_ref, drouter_ref)
+
+
+def expert(x, g, router, mine, win, wout, experts):
     rows, width = x.shape
     ff = win.shape[-1]
     return pl.pallas_call(
-        functools.partial(hidden_kernel, experts),
+        functools.partial(expert_kernel, experts),
         grid=(ff // FF_BLOCK,),
         in_specs=[
             fixed(rows, width), fixed(rows, width), fixed(width, 128), fixed(1, 128),
             in_block(width), out_block(width),
         ],
-        out_specs=[slot_block(rows), slot_block(rows), fixed(rows, width)],
+        out_specs=[
+            slot_block(rows), slot_block(rows), fixed(rows, width),
+            fixed(rows, width), fixed(rows, width), fixed(128, width),
+        ],
         out_shape=[
             jax.ShapeDtypeStruct((rows, ff), BF),
             jax.ShapeDtypeStruct((rows, ff), BF),
             jax.ShapeDtypeStruct((rows, width), BF),
-        ],
+            jax.ShapeDtypeStruct((rows, width), BF),
+            jax.ShapeDtypeStruct((rows, width), BF),
+            jax.ShapeDtypeStruct((128, width), F32),
+        ],
+        scratch_shapes=[pltpu.VMEM((rows, width), F32), pltpu.VMEM((rows, width), F32)],
         compiler_params=pltpu.CompilerParams(vmem_limit_bytes=VMEM_BYTES),
         cost_estimate=pl.CostEstimate(
-            flops=8 * rows * width * ff,
+            flops=16 * rows * width * ff,
             bytes_accessed=4 * width * ff + 4 * rows * ff,
             transcendentals=rows * ff,
         ),
-        name="expert_hidden",
+        name="expert",
     )(x, g, router, mine, win, wout)
 
 
-def gradients_kernel(
-    experts, x_ref, g_ref, router_ref, mine_ref, win_ref, wout_ref, xl_ref, deol_ref, actl_ref,
-    dul_ref, act_ref, du_ref, deo_ref, din_ref, dout_ref, xt, xlt,
-):
+def weights_kernel(parts, *refs):
+    xs, deos, acts, dus = (refs[i * parts : (i + 1) * parts] for i in range(4))
+    din_ref, dout_ref = refs[4 * parts : 4 * parts + 2]
+    turned = refs[4 * parts + 2 :]
+
     @pl.when(pl.program_id(0) == 0)
     def _():
-        gated_cotangent(experts, x_ref, g_ref, router_ref, mine_ref, deo_ref)
-        xt[...] = x_ref[...].T
-        xlt[...] = xl_ref[...].T
-
-    hidden_step(x_ref, deo_ref, win_ref, wout_ref, act_ref, du_ref)
-    din_ref[...] = (dot_n(xlt[...], dul_ref[...]) + dot_n(xt[...], du_ref[...])).astype(BF)
-    dout_ref[...] = (dot_n(actl_ref[...].T, deol_ref[...]) + dot_n(act_ref[...].T, deo_ref[...])).astype(BF)
-
-
-def expert_gradients(x, g, router, mine, win, wout, x_local, deo_local, act_local, du_local, experts):
-    rows, width = x.shape
-    own = x_local.shape[0]
-    ff = win.shape[-1]
+        for t, x in zip(turned, xs):
+            t[...] = x[...].T
+
+    din = [dot_n(t[...], du[...]) for t, du in zip(turned, dus)]
+    dout = [dot_n(act[...].T, deo[...]) for act, deo in zip(acts, deos)]
+    din_ref[...] = sum(din[1:], din[0]).astype(BF)
+    dout_ref[...] = sum(dout[1:], dout[0]).astype(BF)
+
+
+def expert_weights(xs, deos, acts, dus):
+    width = xs[0].shape[1]
+    ff = acts[0].shape[1]
+    parts = len(xs)
+    total = sum(x.shape[0] for x in xs)
     return pl.pallas_call(
-        functools.partial(gradients_kernel, experts),
+        functools.partial(weights_kernel, parts),
         grid=(ff // FF_BLOCK,),
-        in_specs=[
-            fixed(rows, width), fixed(rows, width), fixed(width, 128), fixed(1, 128),
-            in_block(width), out_block(width), fixed(own, width), fixed(own, width),
-            slot_block(own), slot_block(own),
-        ],
+        in_specs=[fixed(*x.shape) for x in xs]
+        + [fixed(*deo.shape) for deo in deos]
+        + [slot_block(act.shape[0]) for act in acts]
+        + [slot_block(du.shape[0]) for du in dus],
         out_specs=[
-            slot_block(rows), slot_block(rows), fixed(rows, width),
             pl.BlockSpec((width, FF_BLOCK), lambda f: (0, f)),
             pl.BlockSpec((FF_BLOCK, width), lambda f: (f, 0)),
         ],
         out_shape=[
-            jax.ShapeDtypeStruct((rows, ff), BF),
-            jax.ShapeDtypeStruct((rows, ff), BF),
-            jax.ShapeDtypeStruct((rows, width), BF),
             jax.ShapeDtypeStruct((width, ff), BF),
             jax.ShapeDtypeStruct((ff, width), BF),
         ],
-        scratch_shapes=[pltpu.VMEM((width, rows), BF), pltpu.VMEM((width, own), BF)],
+        scratch_shapes=[pltpu.VMEM((width, x.shape[0]), BF) for x in xs],
         compiler_params=pltpu.CompilerParams(vmem_limit_bytes=VMEM_BYTES),
         cost_estimate=pl.CostEstimate(
-            flops=12 * (rows + own) * width * ff,
-            bytes_accessed=8 * width * ff + 4 * (rows + own) * ff,
-            transcendentals=rows * ff,
-        ),
-        name="expert_gradients",
-    )(x, g, router, mine, win, wout, x_local, deo_local, act_local, du_local)
-
-
-def results_kernel(
-    experts, x_ref, g_ref, router_ref, mine_ref, win_ref, wout_ref, act_ref, du_ref,
-    geo_ref, dn_ref, drouter_ref, eo, dx,
-):
-    step = pl.program_id(0)
-
-    @pl.when(step == 0)
-    def _():
-        eo[...] = dot_n(act_ref[...], wout_ref[0])
-        dx[...] = dot_t(du_ref[...], win_ref[0])
-
-    @pl.when(step > 0)
-    def _():
-        eo[...] += dot_n(act_ref[...], wout_ref[0])
-        dx[...] += dot_t(du_ref[...], win_ref[0])
-
-    @pl.when(step == pl.num_programs(0) - 1)
-    def _():
-        made = eo[...].astype(BF).astype(F32)
-        mine = mine_ref[...]
-        probs = probabilities(x_ref[...], router_ref[...], experts)
-        gate = jnp.sum(probs * mine, axis=-1, keepdims=True)
-        geo_ref[...] = (gate * made).astype(BF)
-        dgate = jnp.sum(made * g_ref[...].astype(F32), axis=-1, keepdims=True)
-        dprobs = mine * dgate
-        dlog = probs * (dprobs - jnp.sum(probs * dprobs, axis=-1, keepdims=True))
-        dlog = dlog.astype(BF)
-        dn_ref[...] = (dx[...] + dot_t(dlog, router_ref[...])).astype(BF)
-        drouter_ref[...] = dot_n(dlog.T, x_ref[...])
-
-
-def expert_results(x, g, router, mine, win, wout, act, du, experts):
-    rows, width = x.shape
-    ff = win.shape[-1]
-    return pl.pallas_call(
-        functools.partial(results_kernel, experts),
-        grid=(ff // FF_BLOCK,),
-        in_specs=[
-            fixed(rows, width), fixed(rows, width), fixed(width, 128), fixed(1, 128),
-            in_block(width), out_block(width), slot_block(rows), slot_block(rows),
-        ],
-        out_specs=[fixed(rows, width), fixed(rows, width), fixed(128, width)],
-        out_shape=[
-            jax.ShapeDtypeStruct((rows, width), BF),
-            jax.ShapeDtypeStruct((rows, width), BF),
-            jax.ShapeDtypeStruct((128, width), F32),
-        ],
-        scratch_shapes=[pltpu.VMEM((rows, width), F32), pltpu.VMEM((rows, width), F32)],
-        compiler_params=pltpu.CompilerParams(vmem_limit_bytes=VMEM_BYTES),
-        cost_estimate=pl.CostEstimate(
-            flops=8 * rows * width * ff,
-            bytes_accessed=4 * width * ff + 4 * rows * ff,
+            flops=8 * total * width * ff,
+            bytes_accessed=4 * width * ff + 4 * total * ff,
             transcendentals=0,
         ),
-        name="expert_results",
-    )(x, g, router, mine, win, wout, act, du)
+        name="expert_weights",
+    )(*xs, *deos, *acts, *dus)
+
+
+def finish(experts, x_ref, g_ref, router_ref, mine_ref, eo, dx, geo_ref, dn_ref, drouter_ref):
+    made = eo[...].astype(BF).astype(F32)
+    mine = mine_ref[...]
+    probs = probabilities(x_ref[...], router_ref[...], experts)
+    gate = jnp.sum(probs * mine, axis=-1, keepdims=True)
+    geo_ref[...] = (gate * made).astype(BF)
+    dgate = jnp.sum(made * g_ref[...].astype(F32), axis=-1, keepdims=True)
+    dprobs = mine * dgate
+    dlog = probs * (dprobs - jnp.sum(probs * dprobs, axis=-1, keepdims=True))
+    dlog = dlog.astype(BF)
+    dn_ref[...] = (dx[...] + dot_t(dlog, router_ref[...])).astype(BF)
+    drouter_ref[...] = dot_n(dlog.T, x_ref[...])
+
+
 EPS = 1e-06
 NEG = -1e30
 HIGH = lax.Precision.HIGHEST
@@ -412,16 +383,33 @@
     return lax.rem(lax.axis_index(key[0]) // key[1], 2)
 
 
-def gather_bits(value, order, keys, sizes):
-    held = []
-    shape = value.shape
-    for key in order:
-        got = partner(value, key, sizes)
-        at = sum(keys.index(other) < keys.index(key) for other in held)
-        lower = side(key) == 0
-        value = jnp.where(lower, jnp.stack([value, got], at), jnp.stack([got, value], at))
-        held.append(key)
-    return value.reshape((-1,) + shape[1:])
+def gather_direct(value, keys, sizes):
+    ways = sizes["expert"]
+    near = keys.index(("fsdp", 1)) if ("fsdp", 1) in keys else None
+    weights = [bit * (ways if axis == "fsdp" else 1) for axis, bit in keys]
+    count = sizes["fsdp"] * ways
+    far = [w for at, w in enumerate(weights) if at != near]
+    masks = [0]
+    for w in far:
+        masks += [mask | w for mask in masks]
+    me = lax.axis_index("fsdp") * ways + lax.axis_index("expert")
+    blocks = []
+    for mask in masks:
+        got = value
+        if mask:
+            got = lax.ppermute(value, GROUP, [(i, i ^ mask) for i in range(count)])
+        blocks.append((mask, got))
+        if near is not None:
+            mask_near = mask | weights[near]
+            crossed = lax.ppermute(got, GROUP, [(i, i ^ weights[near]) for i in range(count)])
+            blocks.append((mask_near, crossed))
+    blocks = [block for _, block in sorted(blocks, key=lambda item: item[0])]
+    for w in sorted(weights):
+        swapped = lax.rem(me // w, 2) == 1
+        blocks = [
+            jnp.where(swapped, blocks[at ^ w], blocks[at]) for at in range(count)
+        ]
+    return jnp.concatenate(blocks, axis=0)
 
 
 def scatter_bits(value, order, keys, sizes):
@@ -441,19 +429,28 @@
     return lax.ppermute(value, axis, [(i, (i + by) % size) for i in range(size)])
 
 
-def sum_over(value, axis, size):
+def sum_blocks(value, axis, size):
     me = lax.axis_index(axis)
     blocks = value.reshape((size, value.shape[0] // size) + value.shape[1:])
     total = lax.dynamic_index_in_dim(blocks, me, 0, False).astype(F32)
     for s in range(1, size):
         block = lax.dynamic_index_in_dim(blocks, lax.rem(me + s, size), 0, False)
         total = total + shift(block, axis, s, size).astype(F32)
-    total = total.astype(value.dtype)
-    out = lax.dynamic_update_index_in_dim(jnp.zeros_like(blocks), total, me, 0)
+    return total.astype(value.dtype)
+
+
+def spread_blocks(total, axis, size):
+    me = lax.axis_index(axis)
+    out = jnp.zeros((size,) + total.shape, total.dtype)
+    out = lax.dynamic_update_index_in_dim(out, total, me, 0)
     for s in range(1, size):
         got = shift(total, axis, s, size)
         out = lax.dynamic_update_index_in_dim(out, got, lax.rem(me - s + size, size), 0)
-    return out.reshape(value.shape)
+    return out.reshape((size * total.shape[0],) + total.shape[1:])
+
+
+def sum_over(value, axis, size):
+    return spread_blocks(sum_blocks(value, axis, size), axis, size)
 
 
 def swap(blocks, sign, experts):
@@ -513,14 +510,7 @@
     packed = jnp.concatenate(
         [w_query, w_key, w_value] + small_cols + [jnp.zeros((shard, -used % 128), BF)], axis=1
     )
-    half = packed.shape[1] // 256 * 128
-    gathered = jnp.concatenate(
-        [
-            gather_bits(packed[:, :half], others + ways, keys, sizes),
-            gather_bits(packed[:, half:], ways[:-1] + others + ways[-1:], keys, sizes),
-        ],
-        axis=1,
-    )
+    gathered = gather_direct(packed, keys, sizes)
     proj_in = gathered[:, : 3 * inner]
     small = gathered[:, 3 * inner :]
     gain_one = small[:, 0].astype(F32)
@@ -572,22 +562,15 @@
     route_wide = jnp.pad(route_weight, ((0, 0), (0, 128 - experts)))
     mine = (jnp.arange(128, dtype=jnp.int32) == me).astype(F32)[None, :]
     shared = (route_wide, mine, expert_in, expert_out)
-    act_l, du_l, deo_l = expert_hidden(x_local, g_local, *shared, experts)
-    act_r, du_r, deo_r, d_in, d_out = expert_gradients(
-        x_remote, g_remote, *shared, x_local, deo_l, act_l, du_l, experts
-    )
-    sum_in, sum_out = lax.psum((d_in, d_out), ("rep", "fsdp"))
+    act_l, du_l, deo_l, geo_l, dn_l, dr_l = expert(x_local, g_local, *shared, experts)
+    act_r, du_r, deo_r, geo_r, dn_r, dr_r = expert(x_remote, g_remote, *shared, experts)
 
     def cut(rows):
         return [rows[s * capacity : (s + 1) * capacity] for s in range(experts - 1)]
 
-    geo_r, dn_r, dr_r = expert_results(
-        x_remote, g_remote, *shared, after(act_r, d_in), du_r, experts
-    )
     dn_back = swap(cut(dn_r), -1, experts)
-    geo_l, dn_l, dr_l = expert_results(
-        x_local, g_local, *shared, after(act_l, dn_r), du_l, experts
-    )
+    d_in, d_out = expert_weights([x_local, x_remote], [deo_l, deo_r], [act_l, act_r], [du_l, du_r])
+    sum_in, sum_out = lax.psum((d_in, d_out), ("rep", "fsdp"))
     d_second = dot32(to_tokens, jnp.concatenate([dn_l] + dn_back, axis=0))
     geo_back = swap(cut(after(geo_r, dn_back[-1])), -1, experts)
     output = resid + dot32(to_tokens, jnp.concatenate([geo_l] + geo_back, axis=0))
@@ -631,10 +614,9 @@
     )
     order = ways[-1:] + others + ways[:-1]
     share_in, share_out, share_small = [
-        sum_over(scatter_bits(value, order, keys, sizes), "rep", sizes["rep"])
+        sum_over(scatter_bits(value, order, keys, sizes), "rep", sizes["rep"]).astype(F32)
         for value in (d_proj, d_proj_output, d_small)
     ]
-    share_in = share_in.astype(F32)
     return (
         output,
         grad_tokens,
@@ -643,7 +625,7 @@
         share_in[:, :inner],
         share_in[:, inner : 2 * inner],
         share_in[:, 2 * inner :],
-        share_out.astype(F32),
+        share_out,
         share_small[:own_buckets, 2 + experts : used],
         share_small[:, 2 : 2 + experts],
         sum_in.astype(F32)[None],

time: 428 us -> 402 us (0.939)
  waiting for transfers between devices: 106 us -> 91.2 us
  Pallas kernels: 132 us -> 125 us
  other arithmetic: 44 us -> 38.6 us
    ppermute x15 -> x9, waiting for transfers between devices: 54.7 us -> 39.2 us  [partner(): return lax.ppermute(value, axis, [(i, i ^ bit) for i in range(sizes[axis])])]
    ppermute x4, waiting for transfers between devices: 15.4 us -> 2.43 us  [swap(): lax.ppermute(block, 'expert', [(i, (i + sign * (at + 1)) % experts) for i...]
    psum x1, waiting for transfers between devices: 10.2 us -> 18.2 us  [body(): sum_in, sum_out = lax.psum((d_in, d_out), ('rep', 'fsdp'))]
    pallas_call x4 -> x3, Pallas kernels: 71.9 us -> 64.4 us  [the longest x2 43.8 us: expert(): pl.pallas_call(functools.partial(expert_kernel, experts), grid=(ff // FF_...]
    ppermute x0 -> x7, waiting for transfers between devices: none -> 6.56 us  [the longest x3 6.55 us: gather_direct(): got = lax.ppermute(value, GROUP, [(i, i ^ mask) for i in range(count)])]
    select_n x10 -> x0, other arithmetic: 6.03 us -> none  [gather_bits(): jnp.where(lower, jnp.stack([value, got], at), jnp.stack([got, value], at))]
    unnamed x1 -> x8, other arithmetic: 0.07 us -> 5.12 us
    ppermute x15 -> x9, starting transfers between devices: 10.9 us -> 6.99 us  [partner(): return lax.ppermute(value, axis, [(i, i ^ bit) for i in range(sizes[axis])])]
  transfers between devices with their start and end apart: 39 -> 40, of which waited for: 17 -> 17; matrix products, arithmetic and copies ran while one was open for 24% -> 23% of each run, Pallas kernels for 21% -> 26%
where the time goes in v2:
time: 402 us; the launch traced here: 394 us
  Pallas kernels  125 us (31%)
  waiting for transfers between devices  91.2 us (23%)
  matrix products  48.5 us (12%)
  starting transfers between devices  43.5 us (11%)
  other arithmetic  38.6 us (10%)
  local copies, waits for them, and re-layouts  32.5 us (8%)
  between operations  15.3 us (4%)
    pallas_call x2, Pallas kernels, expert(): pl.pallas_call(functools.partial(expert_kernel, experts), grid=(ff // FF_...  43.8 us
    ppermute x9, waiting for transfers between devices, partner(): return lax.ppermute(value, axis, [(i, i ^ bit) for i in range(sizes[axis])])  39.2 us
    pallas_call x1, Pallas kernels, attn_bwd(): pl.pallas_call(functools.partial(attn_bwd_kernel, head ** (-0.5), head),...  32 us
    dot_general x9, matrix products, dot32(): return jnp.dot(left, right, preferred_element_type=F32)  31.9 us
    ppermute x18, starting transfers between devices, shift(): lax.ppermute(value, axis, [(i, (i + by) % size) for i in range(size)])  29 us
    pallas_call x1, Pallas kernels, attn_fwd(): pl.pallas_call(functools.partial(attn_fwd_kernel, head ** (-0.5), head),...  28.4 us
    ppermute x18, waiting for transfers between devices, shift(): lax.ppermute(value, axis, [(i, (i + by) % size) for i in range(size)])  24.8 us
    pallas_call x1, Pallas kernels, expert_weights(): pl.pallas_call(functools.partial(weights_kernel, parts), grid=(ff // FF_B...  20.6 us
  transfers between devices with their start and end apart: 40, of which 17 were waited for; matrix products, arithmetic and copies ran while one was open for 23% of the time, Pallas kernels for 26%

profile of v2, /device:TPU:8, one launch (start us, length us, event | category | flops | bytes accessed | tf_op | source)
XLA Modules:
  0.0 394.3 jit_solution(8001164452241431866)
XLA Ops:
  10.3 1.9 concatenate.30
  12.2 1.5 collective-permute-start.4
  13.7 1.5 collective-permute-start
  15.7 1.6 select_convert_fusion.sq_ref
  17.3 1.6 fusion.52.sk_ref
  18.9 1.7 copy.67
  23.3 2.1 iota_compare_fusion
  25.4 1.7 copy.75
  27.8 4.0 %fusion.44 = bf16[640,768]{1,0:T(8,128)(2,1)} fusion(bf16[1024,768]{1,0:T(8,128)(2,1)} %param.31, pred[1280,1024]{1,0:T(32,128)(4,1)} %iota_compare_fusion), kind=kOutput, calls=%fused_computation.57 | convolution fusion | flops 1007124480 | bytes 3211264 | tf_op jit(solution)/shard_map/dot_general | solution.py:370
  31.8 4.2 %collective-permute-done = bf16[96,2432]{1,0:T(8,128)(2,1)} collective-permute-done((bf16[96,2432]{1,0:T(8,128)(2,1)}, bf16[96,2432]{1,0:T(8,128)(2,1)}, u32[]{:S(2)}, u32[]{:S(2)}) %collective-permute-start) | collective-permute-done | bytes 466976 | tf_op jit(solution)/shard_map/ppermute | solution.py:400
  36.0 2.3 collective-permute-done.2
  38.9 2.3 fusion.38.g_ref
  41.1 1.9 select_dynamic-update-slice_fusion.7
  43.0 1.8 select_dynamic-update-slice_fusion.6
  46.9 1.4 copy-done.14
  49.7 1.5 collective-permute-start.8
  52.0 7.8 %convolution_convert_fusion.q_ref.k_ref.v_ref = bf16[1024,2304]{1,0:T(8,128)(2,1)} fusion(bf16[768,2432]{1,0:T(8,128)(2,1)} %copy-done.14, bf16[1024,768]{0,1:T(8,128)(2,1)S(1)} %copy.67, f32[768]{0:T(1024)S(1)} %get-tuple-element.101, f32[1024]{0:T(1024)S(1)} %get-tuple-element.135), kind=kOutput, calls=%fused_computation.6 | convolution fusion | flops 3629383680 | bytes 9837568 | tf_op jit(solution)/shard_map/dot_general | solution.py:370
  59.7 28.4 %attn_fwd.1 = (bf16[1024,768]{1,0:T(8,128)(2,1)}, f32[1024,768]{1,0:T(8,128)}, bf16[6,2,1024,1024]{3,2,1,0:T(8,128)(2,1)}) custom-call(bf16[1024,2304]{1,0:T(8,128)(2,1)} %convolution_convert_fusion.q_ref.k_ref.v_ref, bf16[1024,2304]{1,0:T(8,128)(2,1)} %convolution_convert_fusion.q_ref.k_ref.v_ref, ...), custom_call_target="tpu_custom_call" | custom-call | flops 16106127360 | bytes 25165824 | tf_op jit(solution)/shard_map/attn_fwd/pallas_call | solution.py:88
  88.1 3.5 multiply_reduce_fusion.2
  92.3 1.5 fusion.41
  93.8 2.4 fusion.35.x_ref.refs_0_
  96.8 22.1 %expert.2 = (bf16[640,3072]{1,0:T(8,128)(2,1)}, bf16[640,3072]{1,0:T(8,128)(2,1)}, bf16[640,768]{1,0:T(8,128)(2,1)}, bf16[640,768]{1,0:T(8,128)(2,1)}, bf16[640,768]{1,0:T(8,128)(2,1)}, /*index=5*/f32[128,768]{1,0:T(8,128)}) custom-call(bf16[640,768]{1,0:T(8,128)(2,1)} %fusion.35.x_ref.refs_0_, bf16[640,768]{1,0:T(8,128)(2,1)} %fusion.38.g_ref, ...), custom_call_target="tpu_custom_call" | custom-call | flops 24159191040 | bytes 17301504 | tf_op jit(solution)/shard_map/expert/pallas_call | solution.py:258
  121.0 21.7 %expert.3 = (bf16[640,3072]{1,0:T(8,128)(2,1)}, bf16[640,3072]{1,0:T(8,128)(2,1)}, bf16[640,768]{1,0:T(8,128)(2,1)}, bf16[640,768]{1,0:T(8,128)(2,1)}, bf16[640,768]{1,0:T(8,128)(2,1)}, /*index=5*/f32[128,768]{1,0:T(8,128)}) custom-call(bf16[640,768]{1,0:T(8,128)(2,1)} %copy-done.33, bf16[640,768]{1,0:T(8,128)(2,1)} %collective-permute-done.8.g_ref, ...), custom_call_target="tpu_custom_call" | custom-call | flops 24159191040 | bytes 17301504 | tf_op jit(solution)/shard_map/expert/pallas_call | solution.py:258
  143.4 20.6 %expert_weights.1 = (bf16[768,3072]{1,0:T(8,128)(2,1)}, bf16[3072,768]{1,0:T(8,128)(2,1)}) custom-call(bf16[640,768]{1,0:T(8,128)(2,1)} %fusion.35.x_ref.refs_0_, bf16[640,768]{1,0:T(8,128)(2,1)} %copy-done.33, bf16[640,768]{1,0:T(8,128)(2,1)} %get-tuple-element.52.refs_2_, bf16[640,768]{1,0:T(8,128)(2,1)} %get-tuple-element.53.refs_3_, ...), custom_call_target="tpu_custom_call" | custom-call | flops 24159191040 | bytes 25165824 | tf_op jit(solution)/shard_map/expert_weights/pallas_call | solution.py:309
  166.2 6.4 %multiply_reduce_fusion = (f32[768]{0:T(1024)}, f32[1024]{0:T(1024)S(1)}, f32[1024,768]{0,1:T(8,128)S(1)}) fusion(f32[1024,768]{0,1:T(8,128)} %copy-done.3, f32[1024]{0:T(1024)S(1)} %copy-done.25, f32[768]{0:T(1024)S(1)} %get-tuple-element.100, bf16[640,768]{1,0:T(8,128)(2,1)} %collective-permute-done.9, bf16[640,768]{1,0:T(8,128)(2,1)} %get-tuple-element.43, ...), kind=kOutput, calls=%fused_computation.24 | convolution fusion | flops 2023225600 | bytes 8275968 | tf_op jit(solution)/shard_map/dot_general | solution.py:370
  173.9 2.6 convolution_convert_fusion.2.do_ref
  176.5 32.0 %attn_bwd.1 = (bf16[1024,768]{1,0:T(8,128)(2,1)}, bf16[1024,768]{1,0:T(8,128)(2,1)}, bf16[1024,768]{1,0:T(8,128)(2,1)}, f32[6,2,2048]{2,1,0:T(2,128)}) custom-call(bf16[1024,2304]{1,0:T(8,128)(2,1)} %convolution_convert_fusion.q_ref.k_ref.v_ref, bf16[1024,2304]{1,0:T(8,128)(2,1)} %convolution_convert_fusion.q_ref.k_ref.v_ref, ...), custom_call_target="tpu_custom_call" | custom-call | flops 1610612736 | bytes 3145728 | tf_op jit(solution)/shard_map/attn_bwd/pallas_call | solution.py:161
  208.6 1.7 constant_dynamic-update-slice_fusion.2
  211.0 1.6 copy-done.15
  212.6 5.8 %fusion.12 = (f32[768]{0:T(1024)S(1)}, f32[1024]{0:T(1024)S(1)}, f32[1024,768]{0,1:T(8,128)}) fusion(bf16[1024,768]{0,1:T(8,128)(2,1)S(1)} %copy.67, f32[1024]{0:T(1024)S(1)} %copy-done.22, f32[768]{0:T(1024)S(1)} %get-tuple-element.101, bf16[1024,2304]{1,0:T(8,128)(2,1)S(1)} %constant_dynamic-update-slice_fusion, bf16[768,2432]{1,0:T(8,128)(2,1)S(1)} %copy-done.15), kind=kOutput, calls=%fused_computation.23 | convolution fusion | flops 3629381888 | bytes 12991488 | tf_op jit(solution)/shard_map/dot_general | solution.py:18
  218.4 5.5 %convolution_convert_fusion.1 = bf16[768,2304]{1,0:T(8,128)(2,1)} fusion(bf16[1024,2304]{1,0:T(8,128)(2,1)S(1)} %constant_dynamic-update-slice_fusion, bf16[1024,768]{0,1:T(8,128)(2,1)S(1)} %copy.67, f32[768]{0:T(1024)S(1)} %get-tuple-element.101, f32[1024]{0:T(1024)S(1)} %copy-done.22), kind=kOutput, calls=%fused_computation.11 | convolution fusion | flops 3628793856 | bytes 9837568 | tf_op jit(solution)/shard_map/dot_general | solution.py:595
  223.9 2.5 convolution_convert_fusion.3
  229.3 1.6 concatenate.40
  231.0 1.4 collective-permute-done.11
  233.5 1.9 dynamic-slice_bitcast_fusion.2
  235.5 16.0 %collective-permute-done.12 = f32[2,96,128]{2,1,0:T(8,128)S(1)} collective-permute-done((f32[2,96,128]{2,1,0:T(8,128)S(1)}, f32[2,96,128]{2,1,0:T(8,128)S(1)}, u32[]{:S(2)}, u32[]{:S(2)}) %collective-permute-start.12) | collective-permute-done | bytes 98336 | tf_op jit(solution)/shard_map/ppermute | solution.py:379
  252.2 3.8 fusion.9
  256.6 2.6 collective-permute-start.15
  259.2 2.5 collective-permute-start.14
  263.0 1.6 copy.85
  265.5 2.7 collective-permute-start.18
  270.8 6.7 %collective-permute-done.30 = bf16[2,96,768]{2,1,0:T(8,128)(2,1)S(1)} collective-permute-done((bf16[2,96,768]{2,1,0:T(8,128)(2,1)S(1)}, bf16[2,96,768]{2,1,0:T(8,128)(2,1)S(1)}, u32[]{:S(2)}, u32[]{:S(2)}) %collective-permute-start.30) | collective-permute-done | bytes 294944 | tf_op jit(solution)/shard_map/ppermute | solution.py:379
  280.9 1.9 collective-permute-done.31
  282.9 2.0 fusion.2
  287.9 1.8 collective-permute-start.34
  290.2 2.9 collective-permute-start.32
  293.1 3.9 add_convert_fusion
  297.0 1.6 copy.84
  299.8 1.5 collective-permute-start.36
  302.4 2.9 collective-permute-done.21
  305.3 1.4 fusion.32
  308.1 10.2 %collective-permute-done.22 = bf16[96,2304]{1,0:T(8,128)(2,1)S(1)} collective-permute-done((bf16[96,2304]{1,0:T(8,128)(2,1)S(1)}, bf16[96,2304]{1,0:T(8,128)(2,1)S(1)}, u32[]{:S(2)}, u32[]{:S(2)}) %collective-permute-start.22) | collective-permute-done | bytes 442400 | tf_op jit(solution)/shard_map/ppermute | solution.py:379
  318.4 3.2 collective-permute-start.25
  321.6 3.4 collective-permute-start.24
  325.1 2.8 collective-permute-start.23
  328.6 6.0 %collective-permute-done.24 = bf16[24,2304]{1,0:T(8,128)(2,1)S(1)} collective-permute-done((bf16[24,2304]{1,0:T(8,128)(2,1)S(1)}, bf16[24,2304]{1,0:T(8,128)(2,1)S(1)}, u32[]{:S(2)}, u32[]{:S(2)}) %collective-permute-start.24) | collective-permute-done | bytes 110624 | tf_op jit(solution)/shard_map/ppermute | solution.py:429
  334.6 6.4 %collective-permute-done.23 = bf16[24,2304]{1,0:T(8,128)(2,1)S(1)} collective-permute-done((bf16[24,2304]{1,0:T(8,128)(2,1)S(1)}, bf16[24,2304]{1,0:T(8,128)(2,1)S(1)}, u32[]{:S(2)}, u32[]{:S(2)}) %collective-permute-start.23) | collective-permute-done | bytes 110624 | tf_op jit(solution)/shard_map/ppermute | solution.py:429
  341.8 2.2 collective-permute-start.27
  344.0 4.4 %collective-permute-done.26 = bf16[24,2304]{1,0:T(8,128)(2,1)S(1)} collective-permute-done((bf16[24,2304]{1,0:T(8,128)(2,1)S(1)}, bf16[24,2304]{1,0:T(8,128)(2,1)S(1)}, u32[]{:S(2)}, u32[]{:S(2)}) %collective-permute-start.26) | collective-permute-done | bytes 110624 | tf_op jit(solution)/shard_map/ppermute | solution.py:429
  348.4 4.0 %collective-permute-done.27 = bf16[24,2304]{1,0:T(8,128)(2,1)S(1)} collective-permute-done((bf16[24,2304]{1,0:T(8,128)(2,1)S(1)}, bf16[24,2304]{1,0:T(8,128)(2,1)S(1)}, u32[]{:S(2)}, u32[]{:S(2)}) %collective-permute-start.27) | collective-permute-done | bytes 110624 | tf_op jit(solution)/shard_map/ppermute | solution.py:429
  352.4 3.3 collective-permute-done.28
  356.8 18.2 %all-reduce.6.cloned.1.call-done = (bf16[1,768,3072]{2,1,0:T(8,128)(2,1)}, bf16[1,3072,768]{2,1,0:T(8,128)(2,1)}) async-done(((bf16[1,768,3072]{2,1,0:T(8,128)(2,1)}, bf16[1,3072,768]{2,1,0:T(8,128)(2,1)}), (bf16[1,768,3072]{2,1,0:T(8,128)(2,1)}, bf16[1,3072,768]{2,1,0:T(8,128)(2,1)})) %all-reduce.6.cloned.1.call-update) | async-done | bytes 9437200 | tf_op jit(solution)/shard_map/psum | solution.py:573
  375.0 7.5 %broadcast_in_dim.126 = f32[1,768,3072]{2,1,0:T(8,128)} convert(bf16[1,768,3072]{2,1,0:T(8,128)(2,1)} %get-tuple-element.104) | non-fusion elementwise | flops 2359296 | bytes 14155776 | tf_op jit(solution)/shard_map/broadcast_in_dim | solution.py:631
  382.6 4.5 %broadcast_in_dim.128 = f32[1,3072,768]{2,1,0:T(8,128)} convert(bf16[1,3072,768]{2,1,0:T(8,128)(2,1)S(1)} %copy-done.1) | non-fusion elementwise | flops 2359296 | bytes 14155776 | tf_op jit(solution)/shard_map/broadcast_in_dim | solution.py:632
  (213 shorter events, 43.3 us)
Async XLA Ops:
  7.2 80.9 %all-gather.2.cloned.1.call-start = ((), (), s32[]{:S(2)}) async-start(), calls=%async_computation | async-start | bytes 1327104 | tf_op jit(solution)/shard_map/all_gather | solution.py:521
  10.2 11.3 %copy-start.19 = (s32[1024,1]{0,1:T(1,128)S(1)}, s32[1024,1]{0,1:T(1,128)}, u32[]{:S(2)}) copy-start(s32[1024,1]{0,1:T(1,128)} %param.19) | copy-start | bytes 12292
  10.3 12.4 %copy-start.31 = (s32[1024]{0:T(1024)S(1)}, s32[1024]{0:T(1024)}, u32[]{:S(2)}) copy-start(s32[1024]{0:T(1024)} %param.20) | copy-start | bytes 12292
  12.2 19.6 %collective-permute-start.4 = (bf16[96,2432]{1,0:T(8,128)(2,1)}, bf16[96,2432]{1,0:T(8,128)(2,1)}, u32[]{:S(2)}, u32[]{:S(2)}) collective-permute-start(bf16[96,2432]{1,0:T(8,128)(2,1)} %concatenate.30), channel_id=1, source_target_pairs={{0,1},{1,0},{2,3},{3,2},{4,5},{5,4},{6,7},{7,6},{8,9},{9,8},{10,11... | collective-permute-start | bytes 1400840 | tf_op jit(solution)/shard_map/ppermute | solution.py:400
  13.7 27.4 %collective-permute-start.6 = (bf16[96,2432]{1,0:T(8,128)(2,1)}, bf16[96,2432]{1,0:T(8,128)(2,1)}, u32[]{:S(2)}, u32[]{:S(2)}) collective-permute-start(bf16[96,2432]{1,0:T(8,128)(2,1)} %concatenate.30), channel_id=1, source_target_pairs={{0,2},{1,3},{2,0},{3,1},{4,6},{5,7},{6,4},{7,5},{8,10},{9,11},{10,... | collective-permute-start | bytes 1400840 | tf_op jit(solution)/shard_map/ppermute | solution.py:404
  13.7 22.3 %collective-permute-start = (bf16[96,2432]{1,0:T(8,128)(2,1)}, bf16[96,2432]{1,0:T(8,128)(2,1)}, u32[]{:S(2)}, u32[]{:S(2)}) collective-permute-start(bf16[96,2432]{1,0:T(8,128)(2,1)} %concatenate.30), channel_id=1, source_target_pairs={{0,5},{1,4},{2,7},{3,6},{4,1},{5,0},{6,3},{7,2},{8,13},{9,12},{10,... | collective-permute-start | bytes 1400840 | tf_op jit(solution)/shard_map/ppermute | solution.py:400
  15.2 23.1 %collective-permute-start.2 = (bf16[96,2432]{1,0:T(8,128)(2,1)}, bf16[96,2432]{1,0:T(8,128)(2,1)}, u32[]{:S(2)}, u32[]{:S(2)}) collective-permute-start(bf16[96,2432]{1,0:T(8,128)(2,1)} %concatenate.30), channel_id=1, source_target_pairs={{0,4},{1,5},{2,6},{3,7},{4,0},{5,1},{6,2},{7,3},{8,12},{9,13},{10,... | collective-permute-start | bytes 1400840 | tf_op jit(solution)/shard_map/ppermute | solution.py:400
  20.6 6.5 %copy-start.29 = (s32[2047]{0:T(1024)S(1)}, s32[2047]{0:T(1024)}, u32[]{:S(2)}) copy-start(s32[2047]{0:T(1024)} %param.18) | copy-start | bytes 24568
  21.6 30.4 %copy-start.21 = (f32[1024]{0:T(1024)}, f32[1024]{0:T(1024)S(1)}, u32[]{:S(2)}) copy-start(f32[1024]{0:T(1024)S(1)} %get-tuple-element.135) | copy-start | bytes 12292
  27.2 21.3 %copy-start.17 = (s32[2048]{0:T(1024)}, s32[2048]{0:T(1024)S(1)}, u32[]{:S(2)}) copy-start(s32[2048]{0:T(1024)S(1)} %pad_add_fusion) | copy-start | bytes 24580
  27.8 11.1 %copy-start.7 = (bf16[1024,768]{1,0:T(8,128)(2,1)S(1)}, bf16[1024,768]{1,0:T(8,128)(2,1)}, u32[]{:S(2)}) copy-start(bf16[1024,768]{1,0:T(8,128)(2,1)} %param.31) | copy-start | bytes 4718596
  27.8 11.1 %copy-start.10 = (pred[1280,1024]{1,0:T(32,128)(4,1)S(1)}, pred[1280,1024]{1,0:T(32,128)(4,1)}, u32[]{:S(2)}) copy-start(pred[1280,1024]{1,0:T(32,128)(4,1)} %iota_compare_fusion) | copy-start | bytes 3932164
  31.8 9.3 %collective-permute-start.5 = (bf16[96,2432]{1,0:T(8,128)(2,1)}, bf16[96,2432]{1,0:T(8,128)(2,1)S(1)}, u32[]{:S(2)}, u32[]{:S(2)}) collective-permute-start(bf16[96,2432]{1,0:T(8,128)(2,1)} %collective-permute-done.4), channel_id=1, source_target_pairs={{0,2},{1,3},{2,0},{3,1},{4,6},{5,7},{6,4},{7,5},{8,10},{9,11},{10,... | collective-permute-start | bytes 1400840 | tf_op jit(solution)/shard_map/ppermute | solution.py:404
  36.0 5.1 %collective-permute-start.1 = (bf16[96,2432]{1,0:T(8,128)(2,1)}, bf16[96,2432]{1,0:T(8,128)(2,1)S(1)}, u32[]{:S(2)}, u32[]{:S(2)}) collective-permute-start(bf16[96,2432]{1,0:T(8,128)(2,1)} %collective-permute-done), channel_id=1, source_target_pairs={{0,2},{1,3},{2,0},{3,1},{4,6},{5,7},{6,4},{7,5},{8,10},{9,11},{10,... | collective-permute-start | bytes 1400840 | tf_op jit(solution)/shard_map/ppermute | solution.py:404
  38.3 2.8 collective-permute-start.3
  49.4 325.6 %all-reduce.6.cloned.1.call-start = ((), (), s32[]{:S(2)}) async-start(), calls=%async_computation.1 | async-start | bytes 18874368 | tf_op jit(solution)/shard_map/psum | solution.py:573
  49.7 69.1 %collective-permute-start.8 = (bf16[640,768]{1,0:T(8,128)(2,1)}, bf16[640,768]{1,0:T(8,128)(2,1)}, u32[]{:S(2)}, u32[]{:S(2)}) collective-permute-start(bf16[640,768]{1,0:T(8,128)(2,1)} %fusion.44), channel_id=1, source_target_pairs={{0,1},{1,0},{2,3},{3,2},{4,5},{5,4},{6,7},{7,6},{8,9},{9,8},{10,11... | collective-permute-start | bytes 2949128 | tf_op jit(solution)/shard_map/ppermute | solution.py:458
  88.1 4.2 %copy-start.11 = (pred[1280,1024]{1,0:T(32,128)(4,1)S(1)}, pred[1280,1024]{1,0:T(32,128)(4,1)}, u32[]{:S(2)}) copy-start(pred[1280,1024]{1,0:T(32,128)(4,1)} %iota_compare_fusion) | copy-start | bytes 3932164
  96.2 23.9 %collective-permute-start.7 = (bf16[640,768]{1,0:T(8,128)(2,1)S(1)}, bf16[640,768]{1,0:T(8,128)(2,1)S(1)}, u32[]{:S(2)}, u32[]{:S(2)}) collective-permute-start(bf16[640,768]{1,0:T(8,128)(2,1)S(1)} %fusion.41), channel_id=1, source_target_pairs={{0,1},{1,0},{2,3},{3,2},{4,5},{5,4},{6,7},{7,6},{8,9},{9,8},{10,11... | collective-permute-start | bytes 2949128 | tf_op jit(solution)/shard_map/ppermute | solution.py:458
  142.8 23.5 %collective-permute-start.9 = (bf16[640,768]{1,0:T(8,128)(2,1)}, bf16[640,768]{1,0:T(8,128)(2,1)}, u32[]{:S(2)}, u32[]{:S(2)}) collective-permute-start(bf16[640,768]{1,0:T(8,128)(2,1)} %get-tuple-element.41), channel_id=1, source_target_pairs={{0,1},{1,0},{2,3},{3,2},{4,5},{5,4},{6,7},{7,6},{8,9},{9,8},{10,11... | collective-permute-start | bytes 2949128 | tf_op jit(solution)/shard_map/ppermute | solution.py:458
  166.2 6.4 %copy-start.4 = (f32[1024,768]{0,1:T(8,128)S(1)}, f32[1024,768]{0,1:T(8,128)}, u32[]{:S(2)}) copy-start(f32[1024,768]{0,1:T(8,128)} %copy-done.3) | copy-start | bytes 9437188
  166.2 6.4 %copy-start.23 = (f32[1024]{0:T(1024)S(1)}, f32[1024]{0:T(1024)}, u32[]{:S(2)}) copy-start(f32[1024]{0:T(1024)} %get-tuple-element.136) | copy-start | bytes 12292
  173.9 49.9 %copy-start = (f32[1024,768]{0,1:T(8,128)}, f32[1024,768]{0,1:T(8,128)S(1)}, u32[]{:S(2)}) copy-start(f32[1024,768]{0,1:T(8,128)S(1)} %subtract_add_fusion) | copy-start | bytes 9437188
  218.4 5.5 %copy-start.6 = (bf16[1024,768]{1,0:T(8,128)(2,1)S(1)}, bf16[1024,768]{1,0:T(8,128)(2,1)}, u32[]{:S(2)}) copy-start(bf16[1024,768]{1,0:T(8,128)(2,1)} %get-tuple-element.36.o_ref) | copy-start | bytes 4718596
  223.9 3.8 copy-start.30
  223.9 4.1 %copy-start.16 = (f32[6,2,2048]{2,1,0:T(2,128)S(1)}, f32[6,2,2048]{2,1,0:T(2,128)}, u32[]{:S(2)}) copy-start(f32[6,2,2048]{2,1,0:T(2,128)} %get-tuple-element.51) | copy-start | bytes 294916
  223.9 4.2 %copy-start.18 = (s32[2048]{0:T(1024)S(1)}, s32[2048]{0:T(1024)}, u32[]{:S(2)}) copy-start(s32[2048]{0:T(1024)} %copy-done.17) | copy-start | bytes 24580
  223.9 4.2 %copy-start.28 = (s32[8,4]{0,1:T(4,128)S(1)}, s32[8,4]{0,1:T(4,128)}, u32[]{:S(2)}) copy-start(s32[8,4]{0,1:T(4,128)} %multiply_add_fusion) | copy-start | bytes 388
  226.3 66.7 %collective-permute-start.10 = (bf16[640,768]{1,0:T(8,128)(2,1)}, bf16[640,768]{1,0:T(8,128)(2,1)}, u32[]{:S(2)}, u32[]{:S(2)}) collective-permute-start(bf16[640,768]{1,0:T(8,128)(2,1)} %get-tuple-element.42), channel_id=1, source_target_pairs={{0,1},{1,0},{2,3},{3,2},{4,5},{5,4},{6,7},{7,6},{8,9},{9,8},{10,11... | collective-permute-start | bytes 2949128 | tf_op jit(solution)/shard_map/ppermute | solution.py:458
  228.4 23.8 %copy-start.20 = (f32[1024]{0:T(1024)S(1)}, f32[1024]{0:T(1024)}, u32[]{:S(2)}) copy-start(f32[1024]{0:T(1024)} %get-tuple-element.134) | copy-start | bytes 12292
  230.9 1.5 collective-permute-start.11
  232.5 19.0 %collective-permute-start.12 = (f32[2,96,128]{2,1,0:T(8,128)S(1)}, f32[2,96,128]{2,1,0:T(8,128)S(1)}, u32[]{:S(2)}, u32[]{:S(2)}) collective-permute-start(f32[2,96,128]{2,1,0:T(8,128)S(1)} %dynamic-slice_bitcast_fusion.10), channel_id=1, source_target_pairs={{0,1},{1,0},{2,3},{3,2},{4,5},{5,4},{6,7},{7,6},{8,9},{9,8},{10,11... | collective-permute-start | bytes 294920 | tf_op jit(solution)/shard_map/ppermute | solution.py:379
  235.5 32.7 %collective-permute-start.29 = (bf16[2,2,96,768]{3,2,1,0:T(8,128)(2,1)}, bf16[2,2,96,768]{3,2,1,0:T(8,128)(2,1)}, u32[]{:S(2)}, u32[]{:S(2)}) collective-permute-start(bf16[2,2,96,768]{3,2,1,0:T(8,128)(2,1)} %dynamic-slice_bitcast_fusion.2), channel_id=1, source_target_pairs={{0,2},{2,0},{4,6},{6,4},{1,3},{3,1},{5,7},{7,5},{8,10},{10,8},{12,... | collective-permute-start | bytes 1769480 | tf_op jit(solution)/shard_map/ppermute | solution.py:379
  251.5 4.6 %collective-permute-start.13 = (f32[96,128]{1,0:T(8,128)S(1)}, f32[96,128]{1,0:T(8,128)S(1)}, u32[]{:S(2)}, u32[]{:S(2)}) collective-permute-start(f32[96,128]{1,0:T(8,128)S(1)} %dynamic-slice_bitcast_fusion.11), channel_id=1, source_target_pairs={{0,4},{2,6},{4,0},{6,2},{1,5},{3,7},{5,1},{7,3},{8,12},{10,14},{12... | collective-permute-start | bytes 147464 | tf_op jit(solution)/shard_map/ppermute | solution.py:379
  252.2 9.5 %copy-start.2 = (bf16[768,2304]{1,0:T(8,128)(2,1)S(1)}, bf16[768,2304]{1,0:T(8,128)(2,1)}, u32[]{:S(2)}) copy-start(bf16[768,2304]{1,0:T(8,128)(2,1)} %convolution_convert_fusion.1) | copy-start | bytes 10616836
  256.1 8.5 %collective-permute-start.16 = (f32[24,128]{1,0:T(8,128)S(1)}, f32[24,128]{1,0:T(8,128)S(1)}, u32[]{:S(2)}, u32[]{:S(2)}) collective-permute-start(f32[24,128]{1,0:T(8,128)S(1)} %get-tuple-element.132), channel_id=1, source_target_pairs={{0,24},{8,0},{16,8},{24,16},{1,25},{9,1},{17,9},{25,17},{2,26},{10... | collective-permute-start | bytes 36872 | tf_op jit(solution)/shard_map/ppermute | solution.py:429
  256.6 8.0 %collective-permute-start.15 = (f32[24,128]{1,0:T(8,128)S(1)}, f32[24,128]{1,0:T(8,128)S(1)}, u32[]{:S(2)}, u32[]{:S(2)}) collective-permute-start(f32[24,128]{1,0:T(8,128)S(1)} %get-tuple-element.133), channel_id=1, source_target_pairs={{0,16},{8,24},{16,0},{24,8},{1,17},{9,25},{17,1},{25,9},{2,18},{10... | collective-permute-start | bytes 36872 | tf_op jit(solution)/shard_map/ppermute | solution.py:429
  259.2 5.4 %collective-permute-start.14 = (f32[24,128]{1,0:T(8,128)S(1)}, f32[24,128]{1,0:T(8,128)S(1)}, u32[]{:S(2)}, u32[]{:S(2)}) collective-permute-start(f32[24,128]{1,0:T(8,128)S(1)} %get-tuple-element.131), channel_id=1, source_target_pairs={{0,8},{8,16},{16,24},{24,0},{1,9},{9,17},{17,25},{25,1},{2,10},{10... | collective-permute-start | bytes 36872 | tf_op jit(solution)/shard_map/ppermute | solution.py:429
  261.7 6.5 %copy-start.12 = (bf16[768,768]{1,0:T(8,128)(2,1)S(1)}, bf16[768,768]{1,0:T(8,128)(2,1)}, u32[]{:S(2)}) copy-start(bf16[768,768]{1,0:T(8,128)(2,1)} %convolution_convert_fusion.3) | copy-start | bytes 3538948
  264.6 18.3 %collective-permute-start.20 = (bf16[2,2,96,2304]{3,2,1,0:T(8,128)(2,1)}, bf16[2,2,96,2304]{3,2,1,0:T(8,128)(2,1)S(1)}, u32[]{:S(2)}, u32[]{:S(2)}) collective-permute-start(bf16[2,2,96,2304]{3,2,1,0:T(8,128)(2,1)} %dynamic-slice_bitcast_fusion), channel_id=1, source_target_pairs={{0,2},{2,0},{4,6},{6,4},{1,3},{3,1},{5,7},{7,5},{8,10},{10,8},{12,... | collective-permute-start | bytes 5308424 | tf_op jit(solution)/shard_map/ppermute | solution.py:379
  264.6 4.8 %collective-permute-start.17 = (f32[24,128]{1,0:T(8,128)S(1)}, f32[24,128]{1,0:T(8,128)S(1)}, u32[]{:S(2)}, u32[]{:S(2)}) collective-permute-start(f32[24,128]{1,0:T(8,128)S(1)} %get-tuple-element.111), channel_id=1, source_target_pairs={{0,8},{8,16},{16,24},{24,0},{1,9},{9,17},{17,25},{25,1},{2,10},{10... | collective-permute-start | bytes 36872 | tf_op jit(solution)/shard_map/ppermute | solution.py:429
  265.5 5.3 %collective-permute-start.18 = (f32[24,128]{1,0:T(8,128)S(1)}, f32[24,128]{1,0:T(8,128)S(1)}, u32[]{:S(2)}, u32[]{:S(2)}) collective-permute-start(f32[24,128]{1,0:T(8,128)S(1)} %get-tuple-element.111), channel_id=1, source_target_pairs={{0,16},{8,24},{16,0},{24,8},{1,17},{9,25},{17,1},{25,9},{2,18},{10... | collective-permute-start | bytes 36872 | tf_op jit(solution)/shard_map/ppermute | solution.py:429
  268.2 10.7 %collective-permute-start.19 = (f32[24,128]{1,0:T(8,128)S(1)}, f32[24,128]{1,0:T(8,128)S(1)}, u32[]{:S(2)}, u32[]{:S(2)}) collective-permute-start(f32[24,128]{1,0:T(8,128)S(1)} %get-tuple-element.111), channel_id=1, source_target_pairs={{0,24},{8,0},{16,8},{24,16},{1,25},{9,1},{17,9},{25,17},{2,26},{10... | collective-permute-start | bytes 36872 | tf_op jit(solution)/shard_map/ppermute | solution.py:429
  269.4 8.1 %collective-permute-start.30 = (bf16[2,96,768]{2,1,0:T(8,128)(2,1)S(1)}, bf16[2,96,768]{2,1,0:T(8,128)(2,1)S(1)}, u32[]{:S(2)}, u32[]{:S(2)}) collective-permute-start(bf16[2,96,768]{2,1,0:T(8,128)(2,1)S(1)} %dynamic-slice_bitcast_fusion.4), channel_id=1, source_target_pairs={{0,1},{1,0},{2,3},{3,2},{4,5},{5,4},{6,7},{7,6},{8,9},{9,8},{10,11... | collective-permute-start | bytes 884744 | tf_op jit(solution)/shard_map/ppermute | solution.py:379
  277.6 5.2 %collective-permute-start.31 = (bf16[96,768]{1,0:T(8,128)(2,1)S(1)}, bf16[96,768]{1,0:T(8,128)(2,1)S(1)}, u32[]{:S(2)}, u32[]{:S(2)}) collective-permute-start(bf16[96,768]{1,0:T(8,128)(2,1)S(1)} %dynamic-slice_bitcast_fusion.6), channel_id=1, source_target_pairs={{0,4},{2,6},{4,0},{6,2},{1,5},{3,7},{5,1},{7,3},{8,12},{10,14},{12... | collective-permute-start | bytes 442376 | tf_op jit(solution)/shard_map/ppermute | solution.py:379
  282.9 4.4 %copy-start.13 = (bf16[96,768]{1,0:T(8,128)(2,1)}, bf16[96,768]{1,0:T(8,128)(2,1)S(1)}, u32[]{:S(2)}) copy-start(bf16[96,768]{1,0:T(8,128)(2,1)S(1)} %fusion.55) | copy-start | bytes 442372
  282.9 10.2 %copy-start.5 = (f32[1024,768]{0,1:T(8,128)S(1)}, f32[1024,768]{0,1:T(8,128)}, u32[]{:S(2)}) copy-start(f32[1024,768]{0,1:T(8,128)} %copy-done.3) | copy-start | bytes 9437188
  282.9 10.2 %copy-start.27 = (s32[1024]{0:T(1024)S(1)}, s32[1024]{0:T(1024)}, u32[]{:S(2)}) copy-start(s32[1024]{0:T(1024)} %copy-done.26) | copy-start | bytes 12292
  282.9 10.1 %copy-start.34 = (bf16[640,768]{1,0:T(8,128)(2,1)S(1)}, bf16[640,768]{1,0:T(8,128)(2,1)}, u32[]{:S(2)}) copy-start(bf16[640,768]{1,0:T(8,128)(2,1)} %get-tuple-element.38) | copy-start | bytes 2949124
  285.9 19.4 %collective-permute-start.21 = (bf16[2,96,2304]{2,1,0:T(8,128)(2,1)}, bf16[2,96,2304]{2,1,0:T(8,128)(2,1)}, u32[]{:S(2)}, u32[]{:S(2)}) collective-permute-start(bf16[2,96,2304]{2,1,0:T(8,128)(2,1)} %dynamic-slice_bitcast_fusion.1), channel_id=1, source_target_pairs={{0,1},{1,0},{2,3},{3,2},{4,5},{5,4},{6,7},{7,6},{8,9},{9,8},{10,11... | collective-permute-start | bytes 2654216 | tf_op jit(solution)/shard_map/ppermute | solution.py:379
  287.9 10.7 %collective-permute-start.34 = (bf16[24,768]{1,0:T(8,128)(2,1)}, bf16[24,768]{1,0:T(8,128)(2,1)S(1)}, u32[]{:S(2)}, u32[]{:S(2)}) collective-permute-start(bf16[24,768]{1,0:T(8,128)(2,1)} %get-tuple-element.129), channel_id=1, source_target_pairs={{0,24},{8,0},{16,8},{24,16},{1,25},{9,1},{17,9},{25,17},{2,26},{10... | collective-permute-start | bytes 110600 | tf_op jit(solution)/shard_map/ppermute | solution.py:429
  289.7 8.9 %collective-permute-start.33 = (bf16[24,768]{1,0:T(8,128)(2,1)S(1)}, bf16[24,768]{1,0:T(8,128)(2,1)S(1)}, u32[]{:S(2)}, u32[]{:S(2)}) collective-permute-start(bf16[24,768]{1,0:T(8,128)(2,1)S(1)} %get-tuple-element.130), channel_id=1, source_target_pairs={{0,16},{8,24},{16,0},{24,8},{1,17},{9,25},{17,1},{25,9},{2,18},{10... | collective-permute-start | bytes 110600 | tf_op jit(solution)/shard_map/ppermute | solution.py:429
  290.2 8.4 %collective-permute-start.32 = (bf16[24,768]{1,0:T(8,128)(2,1)S(1)}, bf16[24,768]{1,0:T(8,128)(2,1)S(1)}, u32[]{:S(2)}, u32[]{:S(2)}) collective-permute-start(bf16[24,768]{1,0:T(8,128)(2,1)S(1)} %get-tuple-element.128), channel_id=1, source_target_pairs={{0,8},{8,16},{16,24},{24,0},{1,9},{9,17},{17,25},{25,1},{2,10},{10... | collective-permute-start | bytes 110600 | tf_op jit(solution)/shard_map/ppermute | solution.py:429
  299.4 8.6 %collective-permute-start.35 = (bf16[24,768]{1,0:T(8,128)(2,1)S(1)}, bf16[24,768]{1,0:T(8,128)(2,1)S(1)}, u32[]{:S(2)}, u32[]{:S(2)}) collective-permute-start(bf16[24,768]{1,0:T(8,128)(2,1)S(1)} %get-tuple-element.107), channel_id=1, source_target_pairs={{0,8},{8,16},{16,24},{24,0},{1,9},{9,17},{17,25},{25,1},{2,10},{10... | collective-permute-start | bytes 110600 | tf_op jit(solution)/shard_map/ppermute | solution.py:429
  299.8 8.2 %collective-permute-start.36 = (bf16[24,768]{1,0:T(8,128)(2,1)S(1)}, bf16[24,768]{1,0:T(8,128)(2,1)S(1)}, u32[]{:S(2)}, u32[]{:S(2)}) collective-permute-start(bf16[24,768]{1,0:T(8,128)(2,1)S(1)} %get-tuple-element.107), channel_id=1, source_target_pairs={{0,16},{8,24},{16,0},{24,8},{1,17},{9,25},{17,1},{25,9},{2,18},{10... | collective-permute-start | bytes 110600 | tf_op jit(solution)/shard_map/ppermute | solution.py:429
  301.3 26.6 %collective-permute-start.37 = (bf16[24,768]{1,0:T(8,128)(2,1)S(1)}, bf16[24,768]{1,0:T(8,128)(2,1)S(1)}, u32[]{:S(2)}, u32[]{:S(2)}) collective-permute-start(bf16[24,768]{1,0:T(8,128)(2,1)S(1)} %get-tuple-element.107), channel_id=1, source_target_pairs={{0,24},{8,0},{16,8},{24,16},{1,25},{9,1},{17,9},{25,17},{2,26},{10... | collective-permute-start | bytes 110600 | tf_op jit(solution)/shard_map/ppermute | solution.py:429
  306.7 11.6 %collective-permute-start.22 = (bf16[96,2304]{1,0:T(8,128)(2,1)S(1)}, bf16[96,2304]{1,0:T(8,128)(2,1)S(1)}, u32[]{:S(2)}, u32[]{:S(2)}) collective-permute-start(bf16[96,2304]{1,0:T(8,128)(2,1)S(1)} %dynamic-slice_bitcast_fusion.3), channel_id=1, source_target_pairs={{0,4},{2,6},{4,0},{6,2},{1,5},{3,7},{5,1},{7,3},{8,12},{10,14},{12... | collective-permute-start | bytes 1327112 | tf_op jit(solution)/shard_map/ppermute | solution.py:379
  318.4 10.2 %collective-permute-start.25 = (bf16[24,2304]{1,0:T(8,128)(2,1)S(1)}, bf16[24,2304]{1,0:T(8,128)(2,1)S(1)}, u32[]{:S(2)}, u32[]{:S(2)}) collective-permute-start(bf16[24,2304]{1,0:T(8,128)(2,1)S(1)} %get-tuple-element.126), channel_id=1, source_target_pairs={{0,24},{8,0},{16,8},{24,16},{1,25},{9,1},{17,9},{25,17},{2,26},{10... | collective-permute-start | bytes 331784 | tf_op jit(solution)/shard_map/ppermute | solution.py:429
  321.6 12.9 %collective-permute-start.24 = (bf16[24,2304]{1,0:T(8,128)(2,1)S(1)}, bf16[24,2304]{1,0:T(8,128)(2,1)S(1)}, u32[]{:S(2)}, u32[]{:S(2)}) collective-permute-start(bf16[24,2304]{1,0:T(8,128)(2,1)S(1)} %get-tuple-element.127), channel_id=1, source_target_pairs={{0,16},{8,24},{16,0},{24,8},{1,17},{9,25},{17,1},{25,9},{2,18},{10... | collective-permute-start | bytes 331784 | tf_op jit(solution)/shard_map/ppermute | solution.py:429
  325.1 15.8 %collective-permute-start.23 = (bf16[24,2304]{1,0:T(8,128)(2,1)S(1)}, bf16[24,2304]{1,0:T(8,128)(2,1)S(1)}, u32[]{:S(2)}, u32[]{:S(2)}) collective-permute-start(bf16[24,2304]{1,0:T(8,128)(2,1)S(1)} %get-tuple-element.125), channel_id=1, source_target_pairs={{0,8},{8,16},{16,24},{24,0},{1,9},{9,17},{17,25},{25,1},{2,10},{10... | collective-permute-start | bytes 331784 | tf_op jit(solution)/shard_map/ppermute | solution.py:429
  341.0 7.4 %collective-permute-start.26 = (bf16[24,2304]{1,0:T(8,128)(2,1)S(1)}, bf16[24,2304]{1,0:T(8,128)(2,1)S(1)}, u32[]{:S(2)}, u32[]{:S(2)}) collective-permute-start(bf16[24,2304]{1,0:T(8,128)(2,1)S(1)} %get-tuple-element.109), channel_id=1, source_target_pairs={{0,8},{8,16},{16,24},{24,0},{1,9},{9,17},{17,25},{25,1},{2,10},{10... | collective-permute-start | bytes 331784 | tf_op jit(solution)/shard_map/ppermute | solution.py:429
  341.8 10.6 %collective-permute-start.27 = (bf16[24,2304]{1,0:T(8,128)(2,1)S(1)}, bf16[24,2304]{1,0:T(8,128)(2,1)S(1)}, u32[]{:S(2)}, u32[]{:S(2)}) collective-permute-start(bf16[24,2304]{1,0:T(8,128)(2,1)S(1)} %get-tuple-element.109), channel_id=1, source_target_pairs={{0,16},{8,24},{16,0},{24,8},{1,17},{9,25},{17,1},{25,9},{2,18},{10... | collective-permute-start | bytes 331784 | tf_op jit(solution)/shard_map/ppermute | solution.py:429
  344.0 11.8 %collective-permute-start.28 = (bf16[24,2304]{1,0:T(8,128)(2,1)S(1)}, bf16[24,2304]{1,0:T(8,128)(2,1)S(1)}, u32[]{:S(2)}, u32[]{:S(2)}) collective-permute-start(bf16[24,2304]{1,0:T(8,128)(2,1)S(1)} %get-tuple-element.109), channel_id=1, source_target_pairs={{0,24},{8,0},{16,8},{24,16},{1,25},{9,1},{17,9},{25,17},{2,26},{10... | collective-permute-start | bytes 331784 | tf_op jit(solution)/shard_map/ppermute | solution.py:429
  375.0 7.5 %copy-start.1 = (bf16[1,3072,768]{2,1,0:T(8,128)(2,1)S(1)}, bf16[1,3072,768]{2,1,0:T(8,128)(2,1)}, u32[]{:S(2)}) copy-start(bf16[1,3072,768]{2,1,0:T(8,128)(2,1)} %get-tuple-element.105) | copy-start | bytes 14155780
  (11 other events, 18.1 us)
Sparse Core Ops, SparseCore 0:
  49.6 29.2 all-gather.1
  165.2 209.8 all-reduce.5
